TPU v7x, 32 devices: a whole 2x2x4 slice. The times are simulated.
32 devices in a mesh: dp: 16 (over z, x, core), tensor: 2 (over y).
Axes of the slice: x: 2, y: 2, z: 4, core: 2. Of those that a mesh axis runs over, the one named last changes fastest.
Arguments:
- tokens: bfloat16 [8192, 1024], P('dp'), may hold values from -6 to 6
- cotangent: bfloat16 [8192, 1024], P('dp'), may hold values from -6 to 6
- segment: int32 [8192], P('dp'), may hold values from 0 to 7, never falling along the last dimension, each value on 1 to 6144 neighbouring positions
- variate: int32 [8192], P('dp'), may hold values from 0 to 3
- time: int32 [8192], P('dp'), may hold values from 0 to 4095
- w_qkv: bfloat16 [3, 1024, 1024], P(None, None, 'tensor'), may hold values from -0.1875 to 0.1875
- w_out: bfloat16 [1024, 1024], P('tensor'), may hold values from -2 to 2
- w_gateup: bfloat16 [2, 1024, 2816], P(None, None, 'tensor'), may hold values from -0.1875 to 0.1875
- w_down: bfloat16 [2816, 1024], P('tensor'), may hold values from -0.109375 to 0.109375
- attn_gain: float32 [1024], replicated, may hold values from 0.5 to 1.5
- mlp_gain: float32 [1024], replicated, may hold values from 0.5 to 1.5
- query_gain: float32 [64], replicated, may hold values from 0.5 to 1.5
- key_gain: float32 [64], replicated, may hold values from 0.5 to 1.5
- var_bias: float32 [2, 16], P(None, 'tensor'), may hold values from -4 to 4
Outputs:
- output: bfloat16 [8192, 1024], P('dp', 'tensor')
- grad_input: float32 [8192, 1024], P('dp', 'tensor')
- grad_qkv: float32 [3, 1024, 1024], P(None, None, 'tensor')
- grad_out: float32 [1024, 1024], P('tensor')
- grad_gateup: float32 [2, 1024, 2816], P(None, None, 'tensor')
- grad_down: float32 [2816, 1024], P('tensor')
- grad_attn_gain: float32 [1024], replicated
- grad_mlp_gain: float32 [1024], replicated
- grad_query_gain: float32 [64], replicated
- grad_key_gain: float32 [64], replicated
- grad_var_bias: float32 [2, 16], P(None, 'tensor')
Inputs may be any that keep to these rules, and one draw needn't show every extreme that they name: `segment`: document numbers never fall along the tokens; all documents lie in the one packed sequence of 8192 tokens, each with at most 6144 tokens.
All inputs are finite; a program needn't handle non-finite values.
Results may differ from a plain program's by a relative error of at most 0.022.
Values may be sent and summed in bfloat16 or wider, within the bound.
A program may use at most 256 MiB of HBM per device.

v0:
```python
import functools

import jax
import jax.numpy as jnp
import numpy as np
from jax import lax
from jax.experimental import pallas as pl
from jax.experimental.layout import Layout, with_layout_constraint
from jax.experimental.pallas import tpu as pltpu
from jax.sharding import PartitionSpec as P

HD = 64
LANES = 128
IDS = 16
EPSILON = 1e-05
LOG2E = 1.4426950408889634
FAR = -30000.0
DOCS = 8
VARS = 4
VAR_AT = HD
SEG_AT = VAR_AT + 3 * VARS
ONE_AT = SEG_AT + DOCS
VMEM = 60 * 1024 * 1024
FEWEST = 512
LAGS = (0, 1, 3, 5, 7, 8)
MESH = pl.DeviceIdType.MESH
WHOLE = pl.BlockSpec(memory_space=pltpu.VMEM)
SCALARS = pl.BlockSpec(memory_space=pltpu.SMEM)
ANYWHERE = pl.BlockSpec(memory_space=pl.ANY)
wide = jnp.float32
low = jnp.bfloat16


def params(**more):
    return pltpu.CompilerParams(vmem_limit_bytes=VMEM, **more)


def lanes_of(x):
    return lax.broadcasted_iota(jnp.int32, x.shape, x.ndim - 1)


def dot_nt(a, b):
    return lax.dot_general(a, b, (((1,), (1,)), ((), ())), preferred_element_type=wide)


def dot_tn(a, b):
    return lax.dot_general(a, b, (((0,), (0,)), ((), ())), preferred_element_type=wide)


def dot_nn(a, b):
    return jnp.dot(a, b, preferred_element_type=wide)


def left_pair(a, b):
    return jnp.where(lanes_of(a) < HD, a, pltpu.roll(b, HD, 1))


def right_pair(a, b):
    return jnp.where(lanes_of(a) < HD, pltpu.roll(a, HD, 1), b)


def swap_halves(x):
    return jnp.where(
        lanes_of(x) % HD < HD // 2,
        pltpu.roll(x, LANES - HD // 2, 1),
        pltpu.roll(x, HD // 2, 1),
    )


def head_mean(x):
    row = lax.broadcasted_iota(jnp.int32, (LANES, LANES), 0) // HD
    column = lax.broadcasted_iota(jnp.int32, (LANES, LANES), 1) // HD
    mix = jnp.where(row == column, 1.0 / HD, 0.0).astype(low)
    high = x.astype(low)
    return dot_nn(high, mix) + dot_nn((x - high.astype(wide)).astype(low), mix)


def features(ids, parts, table):
    index = lax.broadcasted_iota(jnp.int32, (IDS, LANES), 0)
    columns = []
    for part in range(parts):
        segs = jnp.broadcast_to(ids[part : part + 1], (IDS, LANES)).astype(jnp.int32)
        at = IDS // 2 + part
        variates = jnp.broadcast_to(ids[at : at + 1], (IDS, LANES)).astype(jnp.int32)
        by_variate = jnp.where(variates == index, 1.0, 0.0)
        by_document = jnp.where(segs == index - VARS, 1.0, 0.0)
        columns.append(
            jnp.where(index < VARS, by_variate, jnp.where(index < VARS + DOCS, by_document, 1.0))
        )
    return dot_tn(jnp.concatenate(columns, axis=1).astype(low), table)


def table_places():
    row = lax.broadcasted_iota(jnp.int32, (IDS, LANES), 0)
    lane = lax.broadcasted_iota(jnp.int32, (IDS, LANES), 1)
    return row, lane


def hot_variates(row, lane, values):
    kept = jnp.where((lane - VAR_AT) % VARS == row, values, 0.0)
    kept = jnp.where(lane < SEG_AT, kept, 0.0)
    kept = jnp.where(lane >= VAR_AT, kept, 0.0)
    return jnp.where(row < VARS, kept, 0.0)


def of_documents(row, lane, values):
    kept = jnp.where(row >= VARS, values, 0.0)
    kept = jnp.where(row < VARS + DOCS, kept, 0.0)
    kept = jnp.where(lane >= SEG_AT, kept, 0.0)
    return jnp.where(lane < ONE_AT, kept, 0.0)


def key_table():
    row, lane = table_places()
    table = hot_variates(row, lane, 1.0)
    table = table + of_documents(row, lane, jnp.where(lane - SEG_AT == row - VARS, 0.0, FAR))
    one = jnp.where(lane >= ONE_AT, jnp.where(lane < ONE_AT + 3, 1.0, 0.0), 0.0)
    return (table + jnp.where(row == VARS + DOCS, one, 0.0)).astype(low)


def query_table(step):
    row, lane = table_places()
    step = jnp.full((IDS, LANES), step, wide)
    high = step.astype(low).astype(wide)
    mid = (step - high).astype(low).astype(wide)
    part = (lane - VAR_AT) // VARS
    step = jnp.where(part == 0, high, jnp.where(part == 1, mid, step - high - mid))
    table = hot_variates(row, lane, step)
    table = table + of_documents(row, lane, jnp.where(lane - SEG_AT == row - VARS, 1.0, 0.0))
    return table.astype(low)


def project_kernel(
    tokens_ref, w_ref, gain_ref, query_gain_ref, key_gain_ref, cosine_ref, sine_ref, ids_ref,
    message_ref, query_ref, key_ref, normed_ref,
):
    rows = tokens_ref.shape[0]

    @pl.when(pl.program_id(0) == 0)
    def norm():
        x = tokens_ref[...].astype(wide)
        scale = lax.rsqrt(jnp.mean(x * x, axis=1, keepdims=True) + EPSILON)
        normed_ref[...] = (x * scale * gain_ref[...]).astype(low)

    normed = normed_ref[...]

    def turned(raw, gain):
        x = raw * lax.rsqrt(head_mean(raw * raw) + EPSILON) * gain
        return x * cosine_ref[...] + swap_halves(x) * sine_ref[...]

    query_ref[...] = dot_nn(normed, w_ref[0])
    key_ref[...] = dot_nn(normed, w_ref[1])
    values = dot_nn(normed, w_ref[2])
    for pair in range(query_ref.shape[1] // LANES):
        span = slice(pair * LANES, (pair + 1) * LANES)
        one, two = 2 * pair, 2 * pair + 1
        query = turned(query_ref[:, span], query_gain_ref[...])
        key = turned(key_ref[:, span], key_gain_ref[...])
        value = values[:, span]
        message_ref[one, :rows] = left_pair(key, value).astype(low)
        message_ref[two, :rows] = right_pair(key, value).astype(low)
        upper, lower = query[: rows // 2], query[rows // 2 :]
        message_ref[one, rows + IDS :] = left_pair(upper, lower).astype(low)
        message_ref[two, rows + IDS :] = right_pair(upper, lower).astype(low)
        message_ref[one, rows : rows + IDS] = ids_ref[...]
        message_ref[two, rows : rows + IDS] = ids_ref[...]


def project(tokens, w_qkv, gain, query_gain, key_gain, cosine, sine, ids):
    rows, depth = tokens.shape
    width = w_qkv.shape[2]
    size = rows + IDS + rows // 2
    wider = LANES * (1 + (width // LANES + 1) % 2)
    column = pl.BlockSpec((rows, wider), lambda i: (0, i))
    return pl.pallas_call(
        project_kernel,
        grid=(width // wider,),
        in_specs=[
            WHOLE,
            pl.BlockSpec((3, depth, wider), lambda i: (0, 0, i)),
            WHOLE, WHOLE, WHOLE, WHOLE, WHOLE, WHOLE,
        ],
        out_specs=(
            pl.BlockSpec((wider // HD, size, LANES), lambda i: (i, 0, 0)),
            column, column,
            pl.BlockSpec((rows, depth), lambda i: (0, 0)),
        ),
        out_shape=(
            jax.ShapeDtypeStruct((width // HD, size, LANES), low),
            jax.ShapeDtypeStruct((rows, width), wide),
            jax.ShapeDtypeStruct((rows, width), wide),
            jax.ShapeDtypeStruct((rows, depth), low),
        ),
        compiler_params=params(),
    )(tokens, w_qkv, gain, query_gain, key_gain, cosine, sine, ids)


def walk(begin, end, body, largest):
    count = (end - begin) // LANES
    many = largest // LANES

    def step(index, carry):
        body(begin + index * largest, largest)
        return carry

    lax.fori_loop(0, count // many, step, 0)
    size = many // 2
    while size:
        piece = size * LANES
        at = begin + (count // (2 * size)) * (2 * piece)

        @pl.when((count // size) % 2 == 1)
        def rest(at=at, piece=piece):
            body(at, piece)

        size //= 2


def scalar(x):
    return x[0, 0].astype(jnp.int32)


def forward_kernel(
    bias_ref, kv_ref, query_in_ref,
    k_ref, v_ref, q_ref, exact_ref, message_ref, runs_ref, acc_ref, seg_ref, upto_ref, keys_ref,
):
    ranks, heads = kv_ref.shape[:2]
    rows = q_ref.shape[0]
    half = rows // 2
    parts = rows // LANES
    block = pl.program_id(0)
    place = lax.axis_index("dp")
    rank = lax.rem(place, ranks)
    head = place // ranks
    filled = lax.broadcasted_iota(jnp.int32, (IDS // 2, LANES), 0) < parts

    @pl.when(block == 0)
    def prepare():
        keys = key_table()
        for rank_at in range(ranks):
            for head_at in range(heads):
                at = head_at * ranks + rank_at
                ids = kv_ref[rank_at, head_at, rows:, :].astype(wide)
                seg_ref[at] = jnp.where(filled, ids[: IDS // 2], DOCS + 1.0)
                extra = features(ids, parts, keys)
                kv = kv_ref[rank_at, head_at, :rows].astype(wide)
                lane = lanes_of(kv)
                span = pl.ds(at * rows, rows)
                k_ref[span, :] = jnp.where(lane < HD, kv, extra).astype(low)
                one = jnp.where(lane < HD + 3, 1.0, 0.0)
                v_ref[span, :] = jnp.where(lane < HD, pltpu.roll(kv, HD, 1), one).astype(low)
        every = seg_ref[...].reshape(ranks * heads * (IDS // 2), LANES)
        own = jnp.stack([seg_ref[head_at * ranks + rank] for head_at in range(heads)])
        own = own.reshape(heads * (IDS // 2), LANES)
        upto_ref[0, 0] = 0
        upto_ref[1, 0] = 0
        for document in range(DOCS):
            for which, segs in ((0, every), (1, own)):
                count = jnp.sum(jnp.where(segs <= document, 1.0, 0.0), keepdims=True)
                upto_ref[which, document + 1] = scalar(count)
        for at in range(ranks * heads):
            segs = seg_ref[at]
            first = scalar(segs[:1, :1])
            last = scalar(segs[parts - 1 : parts, LANES - 1 :])
            keys_ref[0, at] = upto_ref[0, first] // LANES * LANES
            keys_ref[1, at] = (upto_ref[0, last + 1] + LANES - 1) // LANES * LANES
            runs_ref[0, at] = upto_ref[1, first] // LANES * LANES
            runs_ref[1, at] = (upto_ref[1, last + 1] + LANES - 1) // LANES * LANES

    begin = keys_ref[0, block * ranks + rank]
    end = keys_ref[1, block * ranks + rank]
    queries = query_table((bias_ref[0, head] - bias_ref[1, head]) * LOG2E)
    ids = kv_ref[rank, block, pl.ds(rows, IDS), :].astype(wide)
    extra = features(ids, parts, queries)
    folded = query_in_ref[0].astype(wide)
    head_part = jnp.concatenate([folded, pltpu.roll(folded, HD, 1)], axis=0)
    q_ref[...] = jnp.where(lanes_of(extra) < HD, head_part, extra).astype(low)
    acc_ref[...] = jnp.zeros_like(acc_ref)

    def step(start, size):
        span = pl.ds(pl.multiple_of(start, LANES), size)
        probs = jnp.exp2(dot_nt(q_ref[...], k_ref[span, :])).astype(low)
        acc_ref[...] += dot_nn(probs, v_ref[span, :])

    walk(begin, end, step, 2048)
    total = acc_ref[...]
    row_sum = total[:, HD : HD + 1]
    exact = total / row_sum
    exact_ref[...] = jnp.where(lanes_of(total) < HD, exact, jnp.log2(row_sum))
    message_ref[0] = left_pair(exact[:half], exact[half:]).astype(low)


def forward_attention(bias, kv, query):
    ranks, heads, size = kv.shape[:3]
    rows = size - IDS
    every = ranks * heads * rows
    part = pl.BlockSpec((rows, LANES), lambda i: (i, 0))
    fold = pl.BlockSpec((1, rows // 2, LANES), lambda i: (i, 0, 0))
    return pl.pallas_call(
        forward_kernel,
        grid=(heads,),
        in_specs=[SCALARS, WHOLE, fold],
        out_specs=(WHOLE, WHOLE, part, part, fold, SCALARS),
        scratch_shapes=[
            pltpu.VMEM((rows, LANES), wide),
            pltpu.VMEM((ranks * heads, IDS // 2, LANES), wide),
            pltpu.SMEM((2, DOCS + 1), jnp.int32),
            pltpu.SMEM((2, ranks * heads), jnp.int32),
        ],
        out_shape=(
            jax.ShapeDtypeStruct((every, LANES), low),
            jax.ShapeDtypeStruct((every, LANES), low),
            jax.ShapeDtypeStruct((heads * rows, LANES), low),
            jax.ShapeDtypeStruct((heads * rows, LANES), wide),
            jax.ShapeDtypeStruct((heads, rows // 2, LANES), low),
            jax.ShapeDtypeStruct((2, ranks * heads), jnp.int32),
        ),
        compiler_params=params(),
    )(bias, kv, query)


def split_lanes(column, lane, at):
    high = column.astype(low).astype(wide)
    mid = (column - high).astype(low).astype(wide)
    parts = jnp.where(lane == at, high, jnp.where(lane == at + 1, mid, column - high - mid))
    return jnp.where(lane < at + 3, parts, 0.0)


def backward_kernel(
    runs_ref, k_ref, v_ref, q_in_ref, exact_ref, grad_in_ref, ids_ref,
    kv_ref, message_ref, bias_ref, q_ref, g_ref, kt_ref, dk_ref, dv_ref, dq_ref,
):
    heads, half = grad_in_ref.shape[:2]
    rows = 2 * half
    block = pl.program_id(0)

    @pl.when(block == 0)
    def prepare():
        dq_ref[...] = jnp.zeros_like(dq_ref)
        for head_at in range(heads):
            folded = grad_in_ref[head_at].astype(wide)
            for side in range(2):
                span = pl.ds(head_at * rows + side * half, half)
                grad = folded if side == 0 else pltpu.roll(folded, HD, 1)
                lane = lanes_of(grad)
                grad = jnp.where(lane < HD, grad, 0.0)
                exact = exact_ref[span, :]
                delta = jnp.sum(grad * exact, axis=1, keepdims=True)
                g_ref[span, :] = jnp.where(lane < HD, grad, split_lanes(-delta, lane, HD)).astype(low)
                query = q_in_ref[span, :].astype(wide)
                total = split_lanes(-exact[:, HD : HD + 1], lane, ONE_AT)
                q_ref[span, :] = jnp.where(lane < ONE_AT, query, total).astype(low)

    dk_ref[...] = jnp.zeros_like(dk_ref)
    dv_ref[...] = jnp.zeros_like(dv_ref)
    key = k_ref[...]
    value = v_ref[...]
    kt_ref[...] = key.astype(wide).T.astype(low)

    def step(start, size):
        span = pl.ds(pl.multiple_of(start, LANES), size)
        query = q_ref[span, :]
        grad = g_ref[span, :]
        probs = jnp.exp2(dot_nt(key, query))
        grad_scores = (probs * dot_nt(value, grad)).astype(low)
        dv_ref[...] += dot_nn(probs.astype(low), grad)
        dk_ref[...] += dot_nn(grad_scores, query)
        dq_ref[:, span] += dot_nn(kt_ref[...], grad_scores)

    walk(runs_ref[0, block], runs_ref[1, block], step, 2048)
    kv_ref[0, 0] = left_pair(dk_ref[...] * (1.0 / LOG2E), dv_ref[...]).astype(low)

    @pl.when(block == pl.num_programs(0) - 1)
    def finish():
        same = jnp.zeros((8, LANES), wide)
        every = jnp.zeros((8, LANES), wide)
        index = lax.broadcasted_iota(jnp.int32, (8, LANES), 0)
        for head_at in range(heads):
            ids = ids_ref[head_at].astype(wide)
            for part in range(rows // LANES):
                at = head_at * rows + part * LANES
                by_variate = jnp.where(index < VARS, dq_ref[VAR_AT : VAR_AT + 8, at : at + LANES], 0.0)
                variates = jnp.broadcast_to(
                    ids[IDS // 2 + part : IDS // 2 + part + 1], (8, LANES)
                ).astype(jnp.int32)
                same = same + jnp.where(variates == index, by_variate, 0.0)
                every = every + by_variate
            span = dq_ref[:, head_at * rows : (head_at + 1) * rows].T * HD**-0.5
            message_ref[head_at] = left_pair(span[:half], span[half:]).astype(low)
        bias_ref[0] = same
        bias_ref[1] = every - same


def backward_attention(runs, key, value, query, exact, grad, ids):
    every = key.shape[0]
    heads, half = grad.shape[:2]
    rows = 2 * half
    ranks = every // (heads * rows)
    part = pl.BlockSpec((rows, LANES), lambda i, *_: (i, 0))
    return pl.pallas_call(
        backward_kernel,
        grid_spec=pltpu.PrefetchScalarGridSpec(
            num_scalar_prefetch=1,
            grid=(ranks * heads,),
            in_specs=[part, part, WHOLE, WHOLE, WHOLE, WHOLE],
            out_specs=(
                pl.BlockSpec((1, 1, rows, LANES), lambda i, *_: (i % ranks, i // ranks, 0, 0)),
                WHOLE,
                WHOLE,
            ),
            scratch_shapes=[
                pltpu.VMEM((heads * rows, LANES), low),
                pltpu.VMEM((heads * rows, LANES), low),
                pltpu.VMEM((LANES, rows), low),
                pltpu.VMEM((rows, LANES), wide),
                pltpu.VMEM((rows, LANES), wide),
                pltpu.VMEM((LANES, heads * rows), wide),
            ],
        ),
        out_shape=(
            jax.ShapeDtypeStruct((ranks, heads, rows, LANES), low),
            jax.ShapeDtypeStruct((heads, half, LANES), low),
            jax.ShapeDtypeStruct((2, 8, LANES), wide),
        ),
        compiler_params=params(),
    )(runs, key, value, query, exact, grad, ids)


def out_kernel(landed_ref, *refs):
    tensor, heads, half = landed_ref.shape[:3]
    w_refs, (heads_ref, part_ref, other_ref) = refs[:tensor], refs[tensor:]
    for share in range(tensor):
        to_ref = other_ref if share else heads_ref
        for pair in range(heads // 2):
            one = landed_ref[share, 2 * pair].astype(wide)
            two = landed_ref[share, 2 * pair + 1].astype(wide)
            span = pl.ds(pair * LANES, LANES)
            to_ref[:half, span] = left_pair(one, two).astype(low)
            to_ref[half:, span] = right_pair(one, two).astype(low)
        part = dot_nn(to_ref[...], w_refs[share][...])
        if share:
            part_ref[...] += part
        else:
            part_ref[...] = part


def attention_out(landed, w_outs):
    tensor, heads, half = landed.shape[:3]
    depth = w_outs[0].shape[1]
    return pl.pallas_call(
        out_kernel,
        in_specs=[WHOLE] * (1 + tensor),
        out_specs=(WHOLE, WHOLE),
        out_shape=(
            jax.ShapeDtypeStruct((2 * half, heads * HD), low),
            jax.ShapeDtypeStruct((2 * half, depth), wide),
        ),
        scratch_shapes=[pltpu.VMEM((2 * half, heads * HD), low)],
        compiler_params=params(),
    )(landed, *w_outs)


def grad_heads_kernel(grad_ref, w_ref, message_ref):
    half = message_ref.shape[1]
    for pair in range(message_ref.shape[0] // 2):
        both = dot_nt(grad_ref[...], w_ref[pair * LANES : (pair + 1) * LANES, :])
        message_ref[2 * pair] = left_pair(both[:half], both[half:]).astype(low)
        message_ref[2 * pair + 1] = right_pair(both[:half], both[half:]).astype(low)


def grad_heads_of(grad, w_out):
    return pl.pallas_call(
        grad_heads_kernel,
        in_specs=[WHOLE, WHOLE],
        out_specs=WHOLE,
        out_shape=jax.ShapeDtypeStruct((w_out.shape[0] // HD, grad.shape[0] // 2, LANES), low),
        compiler_params=params(),
    )(grad, w_out)


def unproject_kernel(
    landed_ref, query_ref, key_ref, query_gain_ref, key_gain_ref, cosine_ref, sine_ref,
    grad_ref, gains_ref,
):
    rows = query_ref.shape[0]
    half = rows // 2

    @pl.when(pl.program_id(0) == 0)
    def start():
        gains_ref[...] = jnp.zeros_like(gains_ref)

    def back(turned, raw_ref, gain_ref, at):
        grad = turned * cosine_ref[...] - swap_halves(turned) * sine_ref[...]
        raw = raw_ref[...]
        scale = lax.rsqrt(head_mean(raw * raw) + EPSILON)
        unit = raw * scale
        gains_ref[at : at + 1] += jnp.sum(grad * unit, axis=0, keepdims=True)
        scaled = grad * gain_ref[...]
        return scale * (scaled - unit * head_mean(scaled * unit))

    key_one = landed_ref[0, :rows].astype(wide)
    key_two = landed_ref[1, :rows].astype(wide)
    query_one = landed_ref[0, rows:].astype(wide)
    query_two = landed_ref[1, rows:].astype(wide)
    query = jnp.concatenate(
        [left_pair(query_one, query_two), right_pair(query_one, query_two)], axis=0
    )
    grad_ref[0] = back(query, query_ref, query_gain_ref, 0).astype(low)
    grad_ref[1] = back(left_pair(key_one, key_two), key_ref, key_gain_ref, 1).astype(low)
    grad_ref[2] = right_pair(key_one, key_two).astype(low)


def unproject(landed, raw_query, raw_key, query_gain, key_gain, cosine, sine):
    rows, width = raw_query.shape
    column = pl.BlockSpec((rows, LANES), lambda i: (0, i))
    return pl.pallas_call(
        unproject_kernel,
        grid=(width // LANES,),
        in_specs=[
            pl.BlockSpec((2, rows + rows // 2, LANES), lambda i: (i, 0, 0)),
            column, column, WHOLE, WHOLE, WHOLE, WHOLE,
        ],
        out_specs=(
            pl.BlockSpec((3, rows, LANES), lambda i: (0, 0, i)),
            pl.BlockSpec((8, LANES), lambda i: (0, 0)),
        ),
        out_shape=(
            jax.ShapeDtypeStruct((3, rows, width), low),
            jax.ShapeDtypeStruct((8, LANES), wide),
        ),
        compiler_params=params(),
    )(landed, raw_query, raw_key, query_gain, key_gain, cosine, sine)


def remote(src, dst, send, recv, place):
    return pltpu.make_async_remote_copy(
        src_ref=src, dst_ref=dst, send_sem=send, recv_sem=recv,
        device_id={"dp": place}, device_id_type=MESH,
    )


def greet(heads, ranks, head, rank, with_ranks):
    barrier = pltpu.get_barrier_semaphore()
    for step in range(1, heads):
        place = lax.rem(head + step, heads) * ranks + rank
        pl.semaphore_signal(barrier, inc=1, device_id={"dp": place}, device_id_type=MESH)
    if with_ranks:
        for step in range(1, ranks):
            place = head * ranks + lax.rem(rank + step, ranks)
            pl.semaphore_signal(barrier, inc=1, device_id={"dp": place}, device_id_type=MESH)
    pl.semaphore_wait(barrier, heads - 1 + (ranks - 1 if with_ranks else 0))


def spread_kernel(
    message_ref, kv_ref, query_ref, send_a, recv_a, send_b, recv_b, send_f, recv_f, local, *, ranks
):
    heads = message_ref.shape[0]
    size = kv_ref.shape[2]
    rest = query_ref.shape[1]
    place = lax.axis_index("dp")
    head = place // ranks
    rank = lax.rem(place, ranks)
    greet(heads, ranks, head, rank, True)
    firsts = []
    for step in range(1, heads):
        to = lax.rem(head + step, heads)
        at = to * ranks + rank
        first = remote(
            message_ref.at[to, pl.ds(0, size)], kv_ref.at[rank, head],
            send_a.at[step], recv_a.at[step], at,
        )
        second = remote(
            message_ref.at[to, pl.ds(size, rest)], query_ref.at[head],
            send_b.at[step], recv_b.at[step], at,
        )
        first.start()
        second.start()
        firsts.append((first, second))
    mine = [
        pltpu.make_async_copy(message_ref.at[head, pl.ds(0, size)], kv_ref.at[rank, head], local.at[0]),
        pltpu.make_async_copy(message_ref.at[head, pl.ds(size, rest)], query_ref.at[head], local.at[1]),
    ]
    for copy in mine:
        copy.start()
    onward = []

    def forward(step, source, src):
        for other in range(1, ranks):
            copy = remote(
                src, kv_ref.at[rank, source], send_f.at[step, other], recv_f.at[step, other],
                head * ranks + lax.rem(rank + other, ranks),
            )
            copy.start()
            onward.append(copy)

    forward(0, head, message_ref.at[head, pl.ds(0, size)])
    for step in range(1, heads):
        source = lax.rem(head + heads - step, heads)
        firsts[step - 1][0].wait_recv()
        forward(step, source, kv_ref.at[rank, source])
    for first, second in firsts:
        first.wait_send()
        second.wait()
    for copy in mine + onward:
        copy.wait()


def spread(message, ranks, rows):
    heads, size = message.shape[:2]
    dma = pltpu.SemaphoreType.DMA
    return pl.pallas_call(
        functools.partial(spread_kernel, ranks=ranks),
        in_specs=[ANYWHERE],
        out_specs=(ANYWHERE, ANYWHERE),
        out_shape=(
            jax.ShapeDtypeStruct((ranks, heads, rows + IDS, LANES), low),
            jax.ShapeDtypeStruct((heads, rows // 2, LANES), low),
        ),
        scratch_shapes=[dma((heads,))] * 4 + [dma((heads, ranks))] * 2 + [dma((2,))],
        compiler_params=params(collective_id=0, has_side_effects=True),
    )(message)


def exchange_kernel(message_ref, landed_ref, send, recv, local, *, ranks):
    heads = message_ref.shape[0]
    place = lax.axis_index("dp")
    head = place // ranks
    rank = lax.rem(place, ranks)
    greet(heads, ranks, head, rank, False)
    copies = []
    for step in range(1, heads):
        to = lax.rem(head + step, heads)
        copies.append(
            remote(
                message_ref.at[to], landed_ref.at[head], send.at[step], recv.at[step],
                to * ranks + rank,
            )
        )
        copies[-1].start()
    copies.append(pltpu.make_async_copy(message_ref.at[head], landed_ref.at[head], local))
    copies[-1].start()
    for copy in copies:
        copy.wait()


def exchange(message, ranks, collective_id):
    heads = message.shape[0]
    dma = pltpu.SemaphoreType.DMA
    return pl.pallas_call(
        functools.partial(exchange_kernel, ranks=ranks),
        in_specs=[ANYWHERE],
        out_specs=ANYWHERE,
        out_shape=jax.ShapeDtypeStruct(message.shape, message.dtype),
        scratch_shapes=[dma((heads,)), dma((heads,)), dma],
        compiler_params=params(collective_id=collective_id, has_side_effects=True),
    )(message)


def share_out_kernel(message_ref, landed_ref, send, recv, send_t, recv_t, local, *, ranks, tensor):
    heads = message_ref.shape[0]
    place = lax.axis_index("dp")
    side = lax.axis_index("tensor")
    head = place // ranks
    rank = lax.rem(place, ranks)
    barrier = pltpu.get_barrier_semaphore()
    for step in range(1, tensor):
        to = lax.rem(side + step, tensor)
        pl.semaphore_signal(barrier, inc=1, device_id={"tensor": to}, device_id_type=MESH)
    for step in range(1, heads):
        to = lax.rem(head + step, heads) * ranks + rank
        pl.semaphore_signal(barrier, inc=1, device_id={"dp": to}, device_id_type=MESH)
    pl.semaphore_wait(barrier, heads + tensor - 2)
    copies = []
    for step in range(1, heads):
        to = lax.rem(head + step, heads)
        copies.append(
            remote(
                message_ref.at[to], landed_ref.at[0, head], send.at[step], recv.at[step],
                to * ranks + rank,
            )
        )
        copies[-1].start()
    mine = pltpu.make_async_copy(message_ref.at[head], landed_ref.at[0, head], local)
    mine.start()
    onward = []

    def relay(step, source, src):
        for other in range(1, tensor):
            copy = pltpu.make_async_remote_copy(
                src_ref=src, dst_ref=landed_ref.at[tensor - other, source],
                send_sem=send_t.at[step, other], recv_sem=recv_t.at[step, other],
                device_id={"tensor": lax.rem(side + other, tensor)}, device_id_type=MESH,
            )
            copy.start()
            onward.append(copy)

    relay(0, head, message_ref.at[head])
    for step in range(1, heads):
        source = lax.rem(head + heads - step, heads)
        copies[step - 1].wait_recv()
        relay(step, source, landed_ref.at[0, source])
    for copy in copies:
        copy.wait_send()
    mine.wait()
    for copy in onward:
        copy.wait()


def share_out(message, ranks, tensor):
    heads = message.shape[0]
    dma = pltpu.SemaphoreType.DMA
    return pl.pallas_call(
        functools.partial(share_out_kernel, ranks=ranks, tensor=tensor),
        in_specs=[ANYWHERE],
        out_specs=ANYWHERE,
        out_shape=jax.ShapeDtypeStruct((tensor,) + message.shape, message.dtype),
        scratch_shapes=[dma((heads,))] * 2 + [dma((heads, tensor))] * 2 + [dma],
        compiler_params=params(collective_id=1, has_side_effects=True),
    )(message)


def total_kernel(*refs, arrays, chunks, zs, tensor):
    ins, refs = refs[: arrays + 1], refs[arrays + 1 :]
    outs, refs = refs[: arrays + 1], refs[arrays + 1 :]
    count = len(chunks)
    scratch, refs = refs[: 5 * count], refs[5 * count :]
    near_ref, far_ref, line_ref, side_ref, send, recv, send_z, recv_z, send_s, recv_s = refs
    place = lax.axis_index("dp")
    side = lax.axis_index("tensor")
    core = lax.rem(place, 2)
    x = lax.rem(place // 2, 2)
    z = place // 4
    base = place - core
    core_mate = base + 1 - core
    x_mate = z * 4 + (1 - x) * 2 + core
    z_mates = [lax.rem(z + step, zs) * 4 + x * 2 + core for step in range(1, zs)]

    barrier = pltpu.get_barrier_semaphore()
    for to in [core_mate, x_mate] + z_mates:
        pl.semaphore_signal(barrier, inc=1, device_id={"dp": to}, device_id_type=MESH)
    for step in range(1, tensor):
        to = lax.rem(side + step, tensor)
        pl.semaphore_signal(barrier, inc=1, device_id={"tensor": to}, device_id_type=MESH)
    pl.semaphore_wait(barrier, zs + tensor)
    sent = []
    waits = {}

    def rows_at(at, size):
        return pl.ds(pl.multiple_of(at, 16), size)

    def pieces(chunk):
        index, lead, begin, size = chunks[chunk]
        source = ins[index] if lead is None else ins[index].at[lead]
        target = outs[index] if lead is None else outs[index].at[lead]
        source, target = (ref.at[pl.ds(begin, size)] for ref in (source, target))
        return source, target, size, scratch[5 * chunk : 5 * chunk + 5]

    def go(copy, key):
        copy.start()
        sent.append(copy)
        waits.setdefault(key, []).append(copy)

    def arrived(key):
        for copy in waits[key]:
            copy.wait_recv()

    def halve_core(chunk):
        source, _, size, (first, _, _, _, _) = pieces(chunk)
        go(
            remote(
                source.at[rows_at((1 - core) * (size // 2), size // 2)], first,
                send.at[chunk, 0], recv.at[chunk, 0], core_mate,
            ),
            (chunk, 0),
        )

    def halve_x(chunk):
        source, _, size, (first, half, second, _, _) = pieces(chunk)
        arrived((chunk, 0))
        mine = source[rows_at(core * (size // 2), size // 2), :].astype(wide)
        half[...] = (mine + first[...].astype(wide)).astype(low)
        go(
            remote(
                half.at[rows_at((1 - x) * (size // 4), size // 4)], second,
                send.at[chunk, 1], recv.at[chunk, 1], x_mate,
            ),
            (chunk, 1),
        )

    def part_z(chunk):
        _, _, size, (_, half, second, quarter, third) = pieces(chunk)
        arrived((chunk, 1))
        mine = half[rows_at(x * (size // 4), size // 4), :].astype(wide)
        quarter[...] = (mine + second[...].astype(wide)).astype(low)
        part = size // (4 * zs)
        for step in range(1, zs):
            to = lax.rem(z + step, zs)
            go(
                remote(
                    quarter.at[rows_at(to * part, part)], third.at[step],
                    send_z.at[chunk, 0, step], recv_z.at[chunk, 0, step], z_mates[step - 1],
                ),
                (chunk, 2),
            )

    def spread_z(chunk):
        _, target, size, (_, _, _, quarter, third) = pieces(chunk)
        arrived((chunk, 2))
        part = size // (4 * zs)
        total = quarter[rows_at(z * part, part), :].astype(wide)
        for step in range(1, zs):
            total = total + third[step].astype(wide)
        span = rows_at(core * (size // 2) + x * (size // 4) + z * part, part)
        target[span, :] = total.astype(low)
        for step in range(1, zs):
            go(
                remote(
                    target.at[span], target.at[span],
                    send_z.at[chunk, 1, step], recv_z.at[chunk, 1, step], z_mates[step - 1],
                ),
                (chunk, 3),
            )

    def spread_x(chunk):
        _, target, size, _ = pieces(chunk)
        arrived((chunk, 3))
        span = rows_at(core * (size // 2) + x * (size // 4), size // 4)
        go(
            remote(target.at[span], target.at[span], send.at[chunk, 2], recv.at[chunk, 2], x_mate),
            (chunk, 4),
        )

    def spread_core(chunk):
        _, target, size, _ = pieces(chunk)
        arrived((chunk, 4))
        span = rows_at(core * (size // 2), size // 2)
        go(
            remote(target.at[span], target.at[span], send.at[chunk, 3], recv.at[chunk, 3], core_mate),
            (chunk, 5),
        )

    small = ins[arrays]

    def small_core():
        near_ref[0] = small[...]
        go(remote(near_ref.at[0], near_ref.at[1], send_s.at[0, 0], recv_s.at[0, 0], core_mate), "c")

    def small_x():
        arrived("c")
        far_ref[0] = near_ref[0] + near_ref[1]
        go(remote(far_ref.at[0], far_ref.at[1], send_s.at[1, 0], recv_s.at[1, 0], x_mate), "x")

    def small_z():
        arrived("x")
        line_ref[z] = far_ref[0] + far_ref[1]
        for step in range(1, zs):
            go(
                remote(
                    line_ref.at[z], line_ref.at[z], send_s.at[2, step], recv_s.at[2, step],
                    z_mates[step - 1],
                ),
                "z",
            )

    def small_side():
        arrived("z")
        total = line_ref[0]
        for at in range(1, zs):
            total = total + line_ref[at]
        side_ref[side] = total
        for step in range(1, tensor):
            copy = pltpu.make_async_remote_copy(
                src_ref=side_ref.at[side], dst_ref=side_ref.at[side],
                send_sem=send_s.at[3, step], recv_sem=recv_s.at[3, step],
                device_id={"tensor": lax.rem(side + step, tensor)}, device_id_type=MESH,
            )
            go(copy, "s")

    def small_end():
        if tensor > 1:
            arrived("s")
        total = side_ref[0]
        for at in range(1, tensor):
            total = total + side_ref[at]
        outs[arrays][...] = total

    stages = [halve_core, halve_x, part_z, spread_z, spread_x, spread_core]
    smalls = [small_core, small_x, small_z, small_side, small_end]
    for tick in range(max(count + LAGS[-1], len(smalls))):
        for stage in range(len(stages)):
            if 0 <= tick - LAGS[stage] < count:
                stages[stage](tick - LAGS[stage])
        if tick < len(smalls):
            smalls[tick]()
    for chunk in range(count):
        arrived((chunk, 5))
    for copy in sent:
        copy.wait_send()


def total_sums(arrays, small, dp, tensor):
    zs = dp // 4
    chunks = []
    scratch = []
    for index, array in enumerate(arrays):
        leads = [None] if array.ndim == 2 else list(range(array.shape[0]))
        size, width = array.shape[-2:]
        total, size = size, min(size, max(64 * zs, FEWEST))
        for lead, begin in [(a, b) for a in leads for b in range(0, total, size)]:
            chunks.append((index, lead, begin, size))
            scratch += [
                pltpu.VMEM((size // 2, width), low),
                pltpu.VMEM((size // 2, width), low),
                pltpu.VMEM((size // 4, width), low),
                pltpu.VMEM((size // 4, width), low),
                pltpu.VMEM((zs, size // (4 * zs), width), low),
            ]
    dma = pltpu.SemaphoreType.DMA
    count = len(chunks)
    return pl.pallas_call(
        functools.partial(
            total_kernel, arrays=len(arrays), chunks=tuple(chunks), zs=zs, tensor=tensor
        ),
        in_specs=[WHOLE] * (len(arrays) + 1),
        out_specs=(WHOLE,) * (len(arrays) + 1),
        out_shape=tuple(jax.ShapeDtypeStruct(a.shape, a.dtype) for a in [*arrays, small]),
        scratch_shapes=scratch
        + [
            pltpu.VMEM((2,) + small.shape, wide),
            pltpu.VMEM((2,) + small.shape, wide),
            pltpu.VMEM((zs,) + small.shape, wide),
            pltpu.VMEM((tensor,) + small.shape, wide),
        ]
        + [dma((count, 4))] * 2
        + [dma((count, 2, zs))] * 2
        + [dma((4, max(zs, tensor)))] * 2,
        compiler_params=params(collective_id=4, has_side_effects=True),
    )(*arrays, small)


def collect_kernel(
    kv_ref, query_ref, landed_ref, piece_ref, sum_ref,
    send_p, recv_p, send_a, recv_a, send_b, recv_b, local, *, ranks,
):
    heads, rows = kv_ref.shape[1:3]
    half = query_ref.shape[1]
    place = lax.axis_index("dp")
    head = place // ranks
    rank = lax.rem(place, ranks)
    greet(heads, ranks, head, rank, True)
    order = list(range(1, heads)) + [0]
    pieces = {}
    copies = []
    for step in order:
        to = lax.rem(head + step, heads)
        for other in range(1, ranks):
            partner = lax.rem(rank + other, ranks)
            pieces[step, other] = remote(
                kv_ref.at[partner, to], piece_ref.at[other, to],
                send_p.at[step, other], recv_p.at[step, other], head * ranks + partner,
            )
            pieces[step, other].start()
        if step:
            copies.append(
                remote(
                    query_ref.at[to], landed_ref.at[head, pl.ds(rows, half)],
                    send_b.at[step], recv_b.at[step], to * ranks + rank,
                )
            )
        else:
            copies.append(
                pltpu.make_async_copy(
                    query_ref.at[head], landed_ref.at[head, pl.ds(rows, half)], local.at[0]
                )
            )
        copies[-1].start()
    for step in order:
        to = lax.rem(head + step, heads)
        total = kv_ref[rank, to].astype(wide)
        for other in range(1, ranks):
            pieces[step, other].wait_recv()
            total = total + piece_ref[other, to].astype(wide)
        sum_ref[to] = total.astype(low)
        if step:
            copies.append(
                remote(
                    sum_ref.at[to], landed_ref.at[head, pl.ds(0, rows)],
                    send_a.at[step], recv_a.at[step], to * ranks + rank,
                )
            )
        else:
            copies.append(
                pltpu.make_async_copy(
                    sum_ref.at[head], landed_ref.at[head, pl.ds(0, rows)], local.at[1]
                )
            )
        copies[-1].start()
    for piece in pieces.values():
        piece.wait_send()
    for copy in copies:
        copy.wait()


def collect(kv, query):
    ranks, heads, rows = kv.shape[:3]
    dma = pltpu.SemaphoreType.DMA
    return pl.pallas_call(
        functools.partial(collect_kernel, ranks=ranks),
        in_specs=[WHOLE, WHOLE],
        out_specs=ANYWHERE,
        out_shape=jax.ShapeDtypeStruct((heads, rows + rows // 2, LANES), low),
        scratch_shapes=[
            pltpu.VMEM((ranks, heads, rows, LANES), low),
            pltpu.VMEM((heads, rows, LANES), low),
        ]
        + [dma((heads, ranks))] * 2
        + [dma((heads,))] * 4
        + [dma((2,))],
        compiler_params=params(collective_id=3, has_side_effects=True),
    )(kv, query)


def tables(times):
    half = HD // 2
    lane = np.arange(LANES)
    inverse = (10000.0 ** (-2.0 * (lane % half) / HD)).astype(np.float32)
    sign = np.where(lane % HD < half, -1.0, 1.0).astype(np.float32)
    angles = times.astype(wide)[:, None] * inverse[None, :]
    return jnp.cos(angles), jnp.sin(angles) * sign[None, :]


def keep_order(x):
    return with_layout_constraint(x, Layout(major_to_minor=tuple(range(x.ndim))))


def id_rows(x):
    rows = x.reshape(-1, LANES).astype(low)
    return jnp.pad(rows, ((0, IDS // 2 - rows.shape[0]), (0, 0)))


def shards(
    tokens,
    cotangent,
    segment,
    variate,
    time,
    w_qkv,
    w_out,
    w_gateup,
    w_down,
    attn_gain,
    mlp_gain,
    query_gain,
    key_gain,
    var_bias,
):
    rows = tokens.shape[0]
    local_width = w_qkv.shape[2]
    heads = local_width // HD
    dp = lax.axis_size("dp")
    tensor = lax.axis_size("tensor")
    ranks = dp // heads
    place = lax.axis_index("dp")
    head_here = place // ranks
    rank_here = lax.rem(place, ranks)
    width_share = tokens.shape[1] // tensor
    tensor_start = lax.axis_index("tensor") * width_share

    def tensor_sum(x, x_low):
        if tensor == 2:
            return x + lax.ppermute(x_low, "tensor", [(0, 1), (1, 0)]).astype(wide)
        return lax.psum(x_low, "tensor").astype(wide)

    def tensor_share(x):
        mine = lax.dynamic_slice_in_dim(x, tensor_start, width_share, 1)
        if tensor == 2:
            other = lax.dynamic_slice_in_dim(x, width_share - tensor_start, width_share, 1)
            return mine + lax.ppermute(other.astype(low), "tensor", [(0, 1), (1, 0)]).astype(wide)
        return lax.psum_scatter(x, "tensor", scatter_dimension=1, tiled=True)

    cosine, sine = tables(time)
    pair_gain = lambda gain: jnp.concatenate([gain, gain])[None, :]
    ids = jnp.concatenate([id_rows(segment), id_rows(variate)])
    w_outs = [w_out] + [
        lax.ppermute(w_out, "tensor", [((i + step) % tensor, i) for i in range(tensor)])
        for step in range(1, tensor)
    ]
    message, raw_query, raw_key, normed_one = project(
        tokens, w_qkv, attn_gain[None, :], pair_gain(query_gain * (LOG2E * HD**-0.5)),
        pair_gain(key_gain), cosine, sine, ids,
    )
    kv, query_in = spread(message, ranks, rows)
    key_op, value_op, query_op, exact, out_message, runs = forward_attention(
        var_bias, kv, query_in
    )
    heads_out, attn_total = attention_out(share_out(out_message, ranks, tensor), w_outs)
    inputs = tokens.astype(wide)
    middle = inputs + attn_total
    scale_two = lax.rsqrt(jnp.mean(middle * middle, axis=1, keepdims=True) + EPSILON)
    unit_two = middle * scale_two
    normed_two = (unit_two * mlp_gain).astype(low)
    gate_up = jnp.einsum("td,kdf->ktf", normed_two, w_gateup, preferred_element_type=wide)
    gate_vals = gate_up[0]
    up_vals = gate_up[1]
    sig_gate = jax.nn.sigmoid(gate_vals)
    act_gate = gate_vals * sig_gate
    hidden = (act_gate * up_vals).astype(low)
    mlp_part = jnp.dot(hidden, w_down, preferred_element_type=wide)
    grad_hidden = jnp.einsum("te,fe->tf", cotangent, w_down, preferred_element_type=wide)
    grad_gate = grad_hidden * up_vals * sig_gate * (1.0 + gate_vals * (1.0 - sig_gate))
    grad_up = grad_hidden * act_gate
    grad_gu = jnp.stack([grad_gate, grad_up]).astype(low)
    grad_normed_two = jnp.einsum("ktf,kdf->td", grad_gu, w_gateup, preferred_element_type=wide)
    mlp_gain_part = jnp.sum(grad_normed_two * unit_two, axis=0)
    scaled_two = grad_normed_two * mlp_gain
    middle_part = scale_two * (
        scaled_two - unit_two * jnp.mean(scaled_two * unit_two, axis=1, keepdims=True)
    )
    middle_low, hidden_late, grad_gu_late = lax.optimization_barrier(
        (middle_part.astype(low), hidden, grad_gu)
    )
    grad_down = jnp.einsum("tf,te->fe", hidden_late, cotangent, preferred_element_type=wide)
    grad_gateup = jnp.einsum("td,ktf->kdf", normed_two, grad_gu_late, preferred_element_type=wide)
    early = (keep_order(grad_gateup.astype(low)), grad_down.astype(low))
    grad_middle = cotangent.astype(wide) + tensor_sum(middle_part, middle_low)
    grad_middle_low = grad_middle.astype(low)
    grad_middle_low, mlp_part = lax.optimization_barrier((grad_middle_low, mlp_part))
    mlp_share = tensor_share(mlp_part)
    output = (lax.dynamic_slice_in_dim(middle, tensor_start, width_share, 1) + mlp_share).astype(low)
    grad_out = jnp.einsum("tc,td->cd", heads_out, grad_middle_low, preferred_element_type=wide)
    early = lax.psum((*early, grad_out.astype(low)), "dp")
    grad_landed = exchange(grad_heads_of(grad_middle_low, w_out), ranks, 2)
    own_ids = lax.dynamic_index_in_dim(kv[:, :, rows:], rank_here, 0, False)
    back_kv, back_query, bias_tiles = backward_attention(
        runs, key_op, value_op, query_op, exact, grad_landed, own_ids
    )
    same_sum = jnp.sum(bias_tiles[0])
    other_sum = jnp.sum(bias_tiles[1])
    grad_projected, gain_tile = unproject(
        collect(back_kv, back_query), raw_query, raw_key, pair_gain(query_gain),
        pair_gain(key_gain), cosine, sine,
    )
    query_gain_part = gain_tile[0, :HD] + gain_tile[0, HD:]
    key_gain_part = gain_tile[1, :HD] + gain_tile[1, HD:]
    scale_one = lax.rsqrt(jnp.mean(inputs * inputs, axis=1, keepdims=True) + EPSILON)
    unit_one = inputs * scale_one
    grad_qkv = jnp.einsum("td,kte->kde", normed_one, grad_projected, preferred_element_type=wide)
    grad_normed_one = jnp.einsum("kte,kde->td", grad_projected, w_qkv, preferred_element_type=wide)
    attn_gain_part = jnp.sum(grad_normed_one * unit_one, axis=0)
    scaled_one = grad_normed_one * attn_gain
    input_part = scale_one * (
        scaled_one - unit_one * jnp.mean(scaled_one * unit_one, axis=1, keepdims=True)
    )
    grad_input = lax.dynamic_slice_in_dim(grad_middle, tensor_start, width_share, 1) + tensor_share(
        input_part
    )
    depth = tokens.shape[1]
    head_slot = lax.axis_index("tensor") * heads + head_here
    hit = (jnp.arange(tensor * heads, dtype=jnp.int32) == head_slot).astype(wide)
    small = jnp.concatenate(
        [attn_gain_part, mlp_gain_part, query_gain_part, key_gain_part]
        + [same_sum * hit, other_sum * hit]
    )
    length = small.shape[0]
    small = jnp.pad(small, (0, -length % (8 * LANES))).reshape(-1, LANES)
    qkv_sum, small = total_sums([grad_qkv.astype(low)], small, dp, tensor)
    small = small.reshape(-1)[:length]
    gains, biases = small[: 2 * depth + 2 * HD], small[2 * depth + 2 * HD :]
    bias_sum = lax.dynamic_slice_in_dim(
        biases.reshape(2, tensor * heads), lax.axis_index("tensor") * heads, heads, 1
    )
    return (
        output,
        grad_input,
        qkv_sum.astype(wide),
        early[2].astype(wide),
        early[0].astype(wide),
        early[1].astype(wide),
        gains[:depth],
        gains[depth : 2 * depth],
        gains[2 * depth : 2 * depth + HD],
        gains[2 * depth + HD :],
        bias_sum,
    )


def solution(mesh):
    placed = (
        P("dp", None),
        P("dp", None),
        P("dp"),
        P("dp"),
        P("dp"),
        P(None, None, "tensor"),
        P("tensor", None),
        P(None, None, "tensor"),
        P("tensor", None),
        P(),
        P(),
        P(),
        P(),
        P(None, "tensor"),
    )
    return jax.shard_map(
        shards,
        mesh=mesh,
        in_specs=placed,
        out_specs=(
            P("dp", "tensor"),
            P("dp", "tensor"),
            P(None, None, "tensor"),
            P("tensor", None),
            P(None, None, "tensor"),
            P("tensor", None),
            P(),
            P(),
            P(),
            P(),
            P(None, "tensor"),
        ),
        check_vma=False,
    )
```

profile of v0, /device:TPU:8, one launch (start us, length us, event | category | flops | bytes accessed | tf_op | source)
XLA Modules:
  0.0 455.0 jit_solution(11699105715169603865)
XLA Ops:
  7.2 0.0 copy-start
  7.2 0.0 all-reduce.6.cloned.1.call-start
  7.2 1.6 collective-permute-start
  8.8 0.7 convert_element_type.88
  9.5 0.7 broadcast_multiply_fusion.2
  10.2 1.3 maximum_bitcast_fusion
  11.5 0.7 convert_bitcast_fusion.2
  12.2 0.6 fusion.19.ids_ref
  12.8 2.5 fusion.14
  15.3 7.3 %shard_map.239 = (bf16[8,784,128]{2,1,0:T(8,128)(2,1)}, f32[512,512]{1,0:T(8,128)}, f32[512,512]{1,0:T(8,128)}, bf16[512,1024]{1,0:T(8,128)(2,1)}) custom-call(bf16[512,1024]{1,0:T(8,128)(2,1)} %tokens_ref.1, bf16[3,1024,512]{2,1,0:T(8,128)(2,1)} %w_ref.2, f32[1,1024]{1,0:T(1,128)} %bitcast.98, f32[1,128]{1,0:T(1,128)} %get-tuple-element.92.query_gain_ref, ...), custom_call_target="tpu_custom_call" | custom-call | tf_op jit(solution)/shard_map/pallas_call | solution.py:175
  22.6 38.6 %shard_map.240 = (bf16[2,8,528,128]{3,2,1,0:T(8,128)(2,1)}, bf16[8,256,128]{2,1,0:T(8,128)(2,1)}) custom-call(bf16[8,784,128]{2,1,0:T(8,128)(2,1)} %get-tuple-element.37.message_ref), custom_call_target="tpu_custom_call" | custom-call | tf_op jit(solution)/shard_map/pallas_call | solution.py:611
  61.2 36.6 %shard_map.241 = (bf16[8192,128]{1,0:T(8,128)(2,1)}, bf16[8192,128]{1,0:T(8,128)(2,1)}, bf16[4096,128]{1,0:T(8,128)(2,1)}, f32[4096,128]{1,0:T(8,128)}, bf16[8,256,128]{2,1,0:T(8,128)(2,1)}, /*index=5*/s32[2,16]{1,0:T(2,128)}) custom-call(f32[2,8]{1,0:T(2,128)} %bias_ref.1, bf16[2,8,528,128]{3,2,1,0:T(8,128)(2,1)} %get-tuple-element.38.kv_ref, ...), custom_call_target="tpu_custom_call" | custom-call | tf_op jit(solution)/shard_map/pallas_call | solution.py:299
  97.8 23.3 %shard_map.242.landed_ref = bf16[2,8,256,128]{3,2,1,0:T(8,128)(2,1)} custom-call(bf16[8,256,128]{2,1,0:T(8,128)(2,1)} %get-tuple-element.40.message_ref), custom_call_target="tpu_custom_call" | custom-call | tf_op jit(solution)/shard_map/pallas_call | solution.py:712
  121.1 4.5 shard_map.243
  125.6 2.1 multiply_reduce_fusion.1
  127.8 0.0 slice-start
  127.8 6.6 %convolution_bitcast_fusion = f32[2,512,1408]{2,1,0:T(8,128)S(1)} fusion(bf16[2,1024,1408]{2,1,0:T(8,128)(2,1)} %param.23, f32[512,1024]{1,0:T(8,128)S(1)} %get-tuple-element.75, f32[1024]{0:T(1024)S(1)} %copy-done.14, f32[512]{0:T(512)S(1)} %add_rsqrt_fusion.1), kind=kOutput, calls=%fused_computation.1 | convolution fusion | flops 2954362880 | bytes 13637632 | tf_op jit(solution)/shard_map/td,kdf->ktf/dot_general | solution.py:1102
  134.5 0.0 slice-start.1
  134.5 3.2 fusion.11
  137.7 3.4 fusion.9
  141.2 0.3 pad_maximum_fusion
  141.5 0.4 fusion.20
  141.9 1.4 collective-permute-start.1
  143.4 3.2 fusion.24
  146.5 3.3 convolution_convert_fusion
  149.8 5.5 %convert_bitcast_fusion = bf16[2,1024,1408]{2,1,0:T(8,128)(2,1)} fusion(bf16[2,512,1408]{2,1,0:T(8,128)(2,1)S(1)} %pad_maximum_fusion, f32[512,1024]{1,0:T(8,128)S(1)} %get-tuple-element.75, f32[1024]{0:T(1024)S(1)} %copy-done.14, f32[512]{0:T(512)S(1)} %add_rsqrt_fusion.1), kind=kOutput, calls=%fused_computation | convolution fusion | flops 2957246464 | bytes 10754048 | tf_op jit(solution)/shard_map/td,ktf->kdf/dot_general | solution.py:1123
  155.3 12.2 %collective-permute-done.1 = bf16[512,1024]{1,0:T(8,128)(2,1)S(1)} collective-permute-done((bf16[512,1024]{1,0:T(8,128)(2,1)S(1)}, bf16[512,1024]{1,0:T(8,128)(2,1)S(1)}, u32[]{:S(2)}, u32[]{:S(2)}) %collective-permute-start.1) | collective-permute-done | bytes 1048608 | tf_op jit(solution)/shard_map/ppermute | solution.py:1071
  167.6 2.1 fusion.22
  169.7 1.7 convolution_convert_fusion.1
  171.4 0.0 all-reduce.6.cloned.1.call-update
  171.4 0.9 slice.64
  172.3 0.6 maximum_bitcast_fusion.2.query_gain_ref
  172.9 0.6 dynamic-slice_bitcast_fusion.ids_ref
  173.5 3.7 shard_map.244.message_ref
  177.2 1.3 dynamic-slice_convert_fusion.1
  178.5 1.4 collective-permute-start.2
  179.9 18.9 %shard_map.245.grad_in_ref = bf16[8,256,128]{2,1,0:T(8,128)(2,1)} custom-call(bf16[8,256,128]{2,1,0:T(8,128)(2,1)} %shard_map.244.message_ref), custom_call_target="tpu_custom_call" | custom-call | tf_op jit(solution)/shard_map/pallas_call | solution.py:649
  198.8 67.8 %shard_map.246 = (bf16[2,8,512,128]{3,2,1,0:T(8,128)(2,1)}, bf16[8,256,128]{2,1,0:T(8,128)(2,1)}, f32[2,8,128]{2,1,0:T(8,128)}) custom-call(s32[2,16]{1,0:T(2,128)} %get-tuple-element.44.runs_ref, bf16[8192,128]{1,0:T(8,128)(2,1)} %get-tuple-element.45.k_ref, bf16[8192,128]{1,0:T(8,128)(2,1)} %get-tuple-element.46.v_ref, ...), custom_call_target="tpu_custom_call" | custom-call | tf_op jit(solution)/shard_map/pallas_call | solution.py:400
  266.5 56.2 %shard_map.247.landed_ref = bf16[8,768,128]{2,1,0:T(8,128)(2,1)} custom-call(bf16[2,8,512,128]{3,2,1,0:T(8,128)(2,1)} %get-tuple-element.50.kv_ref, bf16[8,256,128]{2,1,0:T(8,128)(2,1)} %get-tuple-element.51.query_ref), custom_call_target="tpu_custom_call" | custom-call | tf_op jit(solution)/shard_map/pallas_call | solution.py:1007
  322.8 6.4 %shard_map.248 = (bf16[3,512,512]{2,1,0:T(8,128)(2,1)}, f32[8,128]{1,0:T(8,128)}) custom-call(bf16[8,768,128]{2,1,0:T(8,128)(2,1)} %shard_map.247.landed_ref, f32[512,512]{1,0:T(8,128)} %get-tuple-element.52.query_ref, f32[512,512]{1,0:T(8,128)} %get-tuple-element.53.key_ref, f32[1,128]{1,0:T(1,128)} %maximum_bitcast_fusion.2.query_gain_ref, ...), custom_call_target="tpu_custom_call" | custom-call | tf_op jit(solution)/shard_map/pallas_call | solution.py:516
  329.2 4.5 fusion.7
  333.7 0.5 fusion.6
  334.2 1.3 copy-done.6
  335.6 0.1 dynamic-slice_convert_fusion
  335.6 0.6 collective-permute-start.3
  336.2 0.6 slice_reduce_fusion
  336.8 0.6 compare_select_fusion.1
  337.5 0.7 compare_select_fusion
  338.1 0.1 add_bitcast_fusion
  338.2 0.1 concatenate.20
  338.3 0.6 pad_bitcast_fusion.refs_1_
  338.9 4.9 %convert_bitcast_fusion.1.refs_0_ = bf16[3,1024,512]{2,1,0:T(8,128)(2,1)} fusion(bf16[3,512,512]{2,1,0:T(8,128)(2,1)} %get-tuple-element.54, bf16[512,1024]{1,0:T(8,128)(2,1)S(1)} %copy-done.18), kind=kOutput, calls=%fused_computation.3 | convolution fusion | flops 1612185600 | bytes 5767168 | tf_op jit(solution)/shard_map/td,kte->kde/dot_general | solution.py:1147
  343.8 76.4 %shard_map.249 = (bf16[3,1024,512]{2,1,0:T(8,128)(2,1)}, f32[24,128]{1,0:T(8,128)}) custom-call(bf16[3,1024,512]{2,1,0:T(8,128)(2,1)} %convert_bitcast_fusion.1.refs_0_, f32[24,128]{1,0:T(8,128)} %pad_bitcast_fusion.refs_1_), custom_call_target="tpu_custom_call" | custom-call | tf_op jit(solution)/shard_map/pallas_call | solution.py:920
  420.2 0.8 slice.79
  421.1 0.7 slice_bitcast_fusion.2
  421.8 0.6 fusion.23
  422.3 0.6 constant_dynamic-slice_fusion
  423.0 5.6 %convert_element_type.106 = f32[3,1024,512]{2,1,0:T(8,128)} convert(bf16[3,1024,512]{2,1,0:T(8,128)(2,1)} %get-tuple-element.58) | non-fusion elementwise | flops 1572864 | bytes 9437184 | tf_op jit(solution)/shard_map/convert_element_type | solution.py:1175
  428.6 0.6 slice_bitcast_fusion.3
  429.2 2.2 add_convert_fusion
  431.4 2.3 add_add_fusion.1
  433.7 2.8 convert_element_type.108
  436.5 8.0 %convert_element_type.111 = f32[2,1024,1408]{2,1,0:T(8,128)} convert(bf16[2,1024,1408]{2,1,0:T(8,128)(2,1)} %get-tuple-element.70) | non-fusion elementwise | flops 2883584 | bytes 17301504 | tf_op jit(solution)/shard_map/convert_element_type | solution.py:1177
  444.5 3.2 convert_element_type.113
  (52 shorter events, 0.1 us)
Async XLA Ops:
  7.2 127.3 %copy-start = (bf16[1408,1024]{1,0:T(8,128)(2,1)S(1)}, bf16[1408,1024]{1,0:T(8,128)(2,1)}, u32[]{:S(2)}) copy-start(bf16[1408,1024]{1,0:T(8,128)(2,1)} %param.24) | copy-start | bytes 8650756
  7.2 426.5 %all-reduce.6.cloned.1.call-start = ((), (), s32[]{:S(2)}) async-start(), calls=%async_computation | async-start | bytes 19398656 | tf_op jit(solution)/shard_map/psum | solution.py:1131
  7.2 113.9 %collective-permute-start = (bf16[512,1024]{1,0:T(8,128)(2,1)}, bf16[512,1024]{1,0:T(8,128)(2,1)}, u32[]{:S(2)}, u32[]{:S(2)}) collective-permute-start(bf16[512,1024]{1,0:T(8,128)(2,1)} %w_ref.3), channel_id=1, source_target_pairs={{1,0},{0,1},{3,2},{2,3},{5,4},{4,5},{7,6},{6,7},{9,8},{8,9},{11,10... | collective-permute-start | bytes 3145736 | tf_op jit(solution)/shard_map/ppermute | solution.py:1085
  97.8 27.9 %copy-start.4 = (bf16[512,1024]{1,0:T(8,128)(2,1)S(1)}, bf16[512,1024]{1,0:T(8,128)(2,1)}, u32[]{:S(2)}) copy-start(bf16[512,1024]{1,0:T(8,128)(2,1)} %tokens_ref.1) | copy-start | bytes 3145732
  125.6 2.1 copy-start.14
  127.8 39.8 %copy-start.2 = (f32[512,1024]{1,0:T(8,128)}, f32[512,1024]{1,0:T(8,128)S(1)}, u32[]{:S(2)}) copy-start(f32[512,1024]{1,0:T(8,128)S(1)} %get-tuple-element.75) | copy-start | bytes 6291460
  127.8 6.7 %copy-start.12 = (bf16[512,1024]{1,0:T(8,128)(2,1)S(1)}, bf16[512,1024]{1,0:T(8,128)(2,1)}, u32[]{:S(2)}) copy-start(bf16[512,1024]{1,0:T(8,128)(2,1)} %param.17) | copy-start | bytes 3145732
  127.8 9.9 %slice-start = ((s8[5767168]{0:T(1024)(128)(4,1)}), s8[4194304]{0:T(1024)(128)(4,1)S(1)}, s32[]{:S(2)}) async-start(s8[5767168]{0:T(1024)(128)(4,1)} %bitcast.99), calls=%async_computation.1 | async-start | bytes 8388608
  134.5 3.3 slice-start.1
  141.9 25.6 %collective-permute-start.1 = (bf16[512,1024]{1,0:T(8,128)(2,1)S(1)}, bf16[512,1024]{1,0:T(8,128)(2,1)S(1)}, u32[]{:S(2)}, u32[]{:S(2)}) collective-permute-start(bf16[512,1024]{1,0:T(8,128)(2,1)S(1)} %fusion.20), channel_id=1, source_target_pairs={{0,1},{1,0},{2,3},{3,2},{4,5},{5,4},{6,7},{7,6},{8,9},{9,8},{10,11... | collective-permute-start | bytes 3145736 | tf_op jit(solution)/shard_map/ppermute | solution.py:1071
  155.3 14.4 %copy-start.19 = (bf16[512,512]{1,0:T(8,128)(2,1)S(1)}, bf16[512,512]{1,0:T(8,128)(2,1)}, u32[]{:S(2)}) copy-start(bf16[512,512]{1,0:T(8,128)(2,1)} %get-tuple-element.59) | copy-start | bytes 1572868
  169.7 1.8 copy-start.9
  171.4 0.9 copy-start.20
  178.5 250.8 %collective-permute-start.2 = (bf16[512,512]{1,0:T(8,128)(2,1)S(1)}, bf16[512,512]{1,0:T(8,128)(2,1)}, u32[]{:S(2)}, u32[]{:S(2)}) collective-permute-start(bf16[512,512]{1,0:T(8,128)(2,1)S(1)} %dynamic-slice_convert_fusion.1), channel_id=1, source_target_pairs={{0,1},{1,0},{2,3},{3,2},{4,5},{5,4},{6,7},{7,6},{8,9},{9,8},{10,11... | collective-permute-start | bytes 1572872 | tf_op jit(solution)/shard_map/ppermute | solution.py:1078
  322.8 6.4 %copy-start.5 = (bf16[512,1024]{1,0:T(8,128)(2,1)S(1)}, bf16[512,1024]{1,0:T(8,128)(2,1)}, u32[]{:S(2)}) copy-start(bf16[512,1024]{1,0:T(8,128)(2,1)} %tokens_ref.1) | copy-start | bytes 3145732
  322.8 6.4 %copy-start.15 = (f32[1024]{0:T(1024)S(1)}, f32[1024]{0:T(1024)}, u32[]{:S(2)}) copy-start(f32[1024]{0:T(1024)} %param.25) | copy-start | bytes 12292
  333.7 2.5 copy-start.16
  333.7 4.4 copy-start.17
  333.7 5.2 %copy-start.18 = (bf16[512,1024]{1,0:T(8,128)(2,1)S(1)}, bf16[512,1024]{1,0:T(8,128)(2,1)}, u32[]{:S(2)}) copy-start(bf16[512,1024]{1,0:T(8,128)(2,1)} %get-tuple-element.55) | copy-start | bytes 3145732
  334.2 1.3 copy-start.6
  335.6 95.8 %collective-permute-start.3 = (bf16[512,512]{1,0:T(8,128)(2,1)S(1)}, bf16[512,512]{1,0:T(8,128)(2,1)}, u32[]{:S(2)}, u32[]{:S(2)}) collective-permute-start(bf16[512,512]{1,0:T(8,128)(2,1)S(1)} %dynamic-slice_convert_fusion), channel_id=1, source_target_pairs={{0,1},{1,0},{2,3},{3,2},{4,5},{5,4},{6,7},{7,6},{8,9},{9,8},{10,11... | collective-permute-start | bytes 1572872 | tf_op jit(solution)/shard_map/ppermute | solution.py:1078
  423.0 5.7 %copy-start.13 = (f32[24,128]{1,0:T(8,128)S(1)}, f32[24,128]{1,0:T(8,128)}, u32[]{:S(2)}) copy-start(f32[24,128]{1,0:T(8,128)} %get-tuple-element.62) | copy-start | bytes 36868
  423.0 6.3 %copy-start.3 = (f32[512,1024]{1,0:T(8,128)S(1)}, f32[512,1024]{1,0:T(8,128)}, u32[]{:S(2)}) copy-start(f32[512,1024]{1,0:T(8,128)} %copy-done.2) | copy-start | bytes 6291460
  423.0 6.3 %copy-start.11 = (f32[512,1024]{1,0:T(8,128)S(1)}, f32[512,1024]{1,0:T(8,128)}, u32[]{:S(2)}) copy-start(f32[512,1024]{1,0:T(8,128)} %fusion.24) | copy-start | bytes 6291460
  423.0 8.4 %copy-start.8 = (f32[512,1024]{1,0:T(8,128)S(1)}, f32[512,1024]{1,0:T(8,128)}, u32[]{:S(2)}) copy-start(f32[512,1024]{1,0:T(8,128)} %get-tuple-element.73) | copy-start | bytes 6291460
  428.6 2.8 copy-start.7
  436.5 8.0 %copy-start.10 = (bf16[1408,1024]{1,0:T(8,128)(2,1)S(1)}, bf16[1408,1024]{1,0:T(8,128)(2,1)}, u32[]{:S(2)}) copy-start(bf16[1408,1024]{1,0:T(8,128)(2,1)} %get-tuple-element.71) | copy-start | bytes 8650756
  444.5 3.2 copy-start.1
Sparse Core Ops, SparseCore 0:
  171.5 250.4 all-reduce.5
where the time goes:
time: 462 us; the launch traced here: 455 us
  Pallas kernels  340 us (74%)
  other arithmetic  38.6 us (8%)
  matrix products  36.3 us (8%)
  between operations  14.9 us (3%)
  waiting for transfers between devices  12.3 us (3%)
  local copies, waits for them, and re-layouts  8.29 us (2%)
  starting transfers between devices  5.06 us (1%)
    pallas_call x1, Pallas kernels, total_sums(): pl.pallas_call(functools.partial(total_kernel, arrays=len(arrays), chunks...  76.4 us
    pallas_call x1, Pallas kernels, backward_attention(): pl.pallas_call(backward_kernel, grid_spec=pltpu.PrefetchScalarGridSpec(nu...  67.8 us
    pallas_call x1, Pallas kernels, collect(): pl.pallas_call(functools.partial(collect_kernel, ranks=ranks), in_specs=[...  56.2 us
    pallas_call x1, Pallas kernels, spread(): pl.pallas_call(functools.partial(spread_kernel, ranks=ranks), in_specs=[A...  38.6 us
    pallas_call x1, Pallas kernels, forward_attention(): pl.pallas_call(forward_kernel, grid=(heads,), in_specs=[SCALARS, WHOLE, f...  36.6 us
    pallas_call x1, Pallas kernels, share_out(): pl.pallas_call(functools.partial(share_out_kernel, ranks=ranks, tensor=te...  23.3 us
    pallas_call x1, Pallas kernels, exchange(): pl.pallas_call(functools.partial(exchange_kernel, ranks=ranks), in_specs=...  18.9 us
    ppermute x1, waiting for transfers between devices, tensor_sum(): return x + lax.ppermute(x_low, 'tensor', [(0, 1), (1, 0)]).astype(wide)  12.2 us
  transfers between devices with their start and end apart: 5, of which 1 were waited for; matrix products, arithmetic and copies ran while one was open for 11% of the time, Pallas kernels for 74%

commit v1 on v0

--- a/solution.py
+++ b/solution.py
@@ -130,17 +130,30 @@
     return table.astype(low)
 
 
+def double_gains(pair_ref, query_ref, key_ref):
+    for side in range(2):
+        span = slice(side * HD, (side + 1) * HD)
+        pair_ref[0:1, span] = query_ref[...] * (LOG2E * HD**-0.5)
+        pair_ref[1:2, span] = query_ref[...]
+        pair_ref[2:3, span] = key_ref[...]
+
+
 def project_kernel(
-    tokens_ref, w_ref, gain_ref, query_gain_ref, key_gain_ref, cosine_ref, sine_ref, ids_ref,
-    message_ref, query_ref, key_ref, normed_ref,
+    tokens_ref, w_ref, gain_ref, query_gain_ref, key_gain_ref, cosine_ref, sine_ref, segs_ref, vars_ref,
+    message_ref, query_ref, key_ref, normed_ref, pair_gain_ref, ids_ref,
 ):
     rows = tokens_ref.shape[0]
+    parts = segs_ref.shape[0]
 
     @pl.when(pl.program_id(0) == 0)
     def norm():
         x = tokens_ref[...].astype(wide)
         scale = lax.rsqrt(jnp.mean(x * x, axis=1, keepdims=True) + EPSILON)
         normed_ref[...] = (x * scale * gain_ref[...]).astype(low)
+        double_gains(pair_gain_ref, query_gain_ref, key_gain_ref)
+        ids_ref[...] = jnp.zeros_like(ids_ref)
+        ids_ref[:parts, :] = segs_ref[...].astype(wide)
+        ids_ref[IDS // 2 : IDS // 2 + parts, :] = vars_ref[...].astype(wide)
 
     normed = normed_ref[...]
 
@@ -154,19 +167,19 @@
     for pair in range(query_ref.shape[1] // LANES):
         span = slice(pair * LANES, (pair + 1) * LANES)
         one, two = 2 * pair, 2 * pair + 1
-        query = turned(query_ref[:, span], query_gain_ref[...])
-        key = turned(key_ref[:, span], key_gain_ref[...])
+        query = turned(query_ref[:, span], pair_gain_ref[0:1])
+        key = turned(key_ref[:, span], pair_gain_ref[2:3])
         value = values[:, span]
         message_ref[one, :rows] = left_pair(key, value).astype(low)
         message_ref[two, :rows] = right_pair(key, value).astype(low)
         upper, lower = query[: rows // 2], query[rows // 2 :]
         message_ref[one, rows + IDS :] = left_pair(upper, lower).astype(low)
         message_ref[two, rows + IDS :] = right_pair(upper, lower).astype(low)
-        message_ref[one, rows : rows + IDS] = ids_ref[...]
-        message_ref[two, rows : rows + IDS] = ids_ref[...]
-
-
-def project(tokens, w_qkv, gain, query_gain, key_gain, cosine, sine, ids):
+        message_ref[one, rows : rows + IDS] = ids_ref[...].astype(low)
+        message_ref[two, rows : rows + IDS] = ids_ref[...].astype(low)
+
+
+def project(tokens, w_qkv, gain, query_gain, key_gain, cosine, sine, segs, variates):
     rows, depth = tokens.shape
     width = w_qkv.shape[2]
     size = rows + IDS + rows // 2
@@ -178,7 +191,7 @@
         in_specs=[
             WHOLE,
             pl.BlockSpec((3, depth, wider), lambda i: (0, 0, i)),
-            WHOLE, WHOLE, WHOLE, WHOLE, WHOLE, WHOLE,
+            WHOLE, WHOLE, WHOLE, WHOLE, WHOLE, WHOLE, WHOLE,
         ],
         out_specs=(
             pl.BlockSpec((wider // HD, size, LANES), lambda i: (i, 0, 0)),
@@ -191,8 +204,9 @@
             jax.ShapeDtypeStruct((rows, width), wide),
             jax.ShapeDtypeStruct((rows, depth), low),
         ),
+        scratch_shapes=[pltpu.VMEM((8, LANES), wide), pltpu.VMEM((IDS, LANES), wide)],
         compiler_params=params(),
-    )(tokens, w_qkv, gain, query_gain, key_gain, cosine, sine, ids)
+    )(tokens, w_qkv, gain, query_gain, key_gain, cosine, sine, segs, variates)
 
 
 def walk(begin, end, body, largest):
@@ -426,38 +440,100 @@
     )(runs, key, value, query, exact, grad, ids)
 
 
-def out_kernel(landed_ref, *refs):
+def columns_of(width):
+    if width % LANES:
+        return [(0, width)]
+    return [(at, min(2 * LANES, width - at)) for at in range(0, width, 2 * LANES)]
+
+
+def mlp_kernel(
+    landed_ref, tokens_ref, cotangent_ref, gain_ref, own_out_ref, other_out_ref, gateup_ref, down_ref,
+    heads_ref, middle_ref, normed_ref, hidden_ref, grad_gu_ref, part_ref, part_low_ref, gain_part_ref,
+    others_ref, gateup_in, down_in, sums_ref, copied,
+):
     tensor, heads, half = landed_ref.shape[:3]
-    w_refs, (heads_ref, part_ref, other_ref) = refs[:tensor], refs[tensor:]
+    copies = [
+        pltpu.make_async_copy(gateup_ref, gateup_in, copied.at[0]),
+        pltpu.make_async_copy(down_ref, down_in, copied.at[1]),
+    ]
+    for copy in copies:
+        copy.start()
     for share in range(tensor):
-        to_ref = other_ref if share else heads_ref
+        to_ref = others_ref if share else heads_ref
         for pair in range(heads // 2):
             one = landed_ref[share, 2 * pair].astype(wide)
             two = landed_ref[share, 2 * pair + 1].astype(wide)
             span = pl.ds(pair * LANES, LANES)
             to_ref[:half, span] = left_pair(one, two).astype(low)
             to_ref[half:, span] = right_pair(one, two).astype(low)
-        part = dot_nn(to_ref[...], w_refs[share][...])
         if share:
-            part_ref[...] += part
+            middle_ref[...] += dot_nn(to_ref[...], other_out_ref[share - 1])
         else:
-            part_ref[...] = part
-
-
-def attention_out(landed, w_outs):
+            middle_ref[...] = tokens_ref[...].astype(wide) + dot_nn(to_ref[...], own_out_ref[...])
+
+    def unit_and_scale():
+        middle = middle_ref[...]
+        scale = lax.rsqrt(jnp.mean(middle * middle, axis=1, keepdims=True) + EPSILON)
+        return middle * scale, scale
+
+    normed_ref[...] = (unit_and_scale()[0] * gain_ref[...]).astype(low)
+    for copy in copies:
+        copy.wait()
+    sums_ref[...] = jnp.zeros_like(sums_ref)
+    for at, size in columns_of(hidden_ref.shape[1]):
+        span = slice(at, at + size)
+        w_gate = gateup_in[0, :, span]
+        w_up = gateup_in[1, :, span]
+        gate = dot_nn(normed_ref[...], w_gate)
+        up = dot_nn(normed_ref[...], w_up)
+        grad = dot_nt(cotangent_ref[...], down_in[span, :])
+        sigmoid = 1.0 / (1.0 + jnp.exp(-gate))
+        active = gate * sigmoid
+        hidden_ref[:, span] = (active * up).astype(low)
+        grad_gate = (grad * up * sigmoid * (1.0 + gate * (1.0 - sigmoid))).astype(low)
+        grad_up = (grad * active).astype(low)
+        grad_gu_ref[0, :, span] = grad_gate
+        grad_gu_ref[1, :, span] = grad_up
+        sums_ref[...] += dot_nt(grad_gate, w_gate) + dot_nt(grad_up, w_up)
+    unit, scale = unit_and_scale()
+    sums = sums_ref[...]
+    gain_part = jnp.sum(sums * unit, axis=0, keepdims=True)
+    for row in range(gain_part_ref.shape[0]):
+        gain_part_ref[row : row + 1, :] = gain_part[:, row * LANES : (row + 1) * LANES]
+    scaled = sums * gain_ref[...]
+    part = scale * (scaled - unit * jnp.mean(scaled * unit, axis=1, keepdims=True))
+    part_ref[...] = part
+    part_low_ref[...] = part.astype(low)
+
+
+def out_and_mlp(landed, tokens, cotangent, gain, w_out, w_others, w_gateup, w_down):
     tensor, heads, half = landed.shape[:3]
-    depth = w_outs[0].shape[1]
+    rows, depth = tokens.shape
+    width, units = heads * HD, w_down.shape[0]
+    shape = jax.ShapeDtypeStruct
     return pl.pallas_call(
-        out_kernel,
-        in_specs=[WHOLE] * (1 + tensor),
-        out_specs=(WHOLE, WHOLE),
+        mlp_kernel,
+        in_specs=[WHOLE] * 6 + [ANYWHERE] * 2,
+        out_specs=(WHOLE,) * 8,
         out_shape=(
-            jax.ShapeDtypeStruct((2 * half, heads * HD), low),
-            jax.ShapeDtypeStruct((2 * half, depth), wide),
+            shape((rows, width), low),
+            shape((rows, depth), wide),
+            shape((rows, depth), low),
+            shape((rows, units), low),
+            shape((2, rows, units), low),
+            shape((rows, depth), wide),
+            shape((rows, depth), low),
+            shape((depth // LANES, LANES), wide),
         ),
-        scratch_shapes=[pltpu.VMEM((2 * half, heads * HD), low)],
+        scratch_shapes=[
+            pltpu.VMEM((rows, width), low),
+            pltpu.VMEM(w_gateup.shape, low),
+            pltpu.VMEM(w_down.shape, low),
+            pltpu.VMEM((rows, depth), wide),
+            pltpu.SemaphoreType.DMA((2,)),
+        ],
         compiler_params=params(),
-    )(landed, *w_outs)
+    )(landed, tokens, cotangent, gain, w_out, w_others, w_gateup, w_down)
 
 
 def grad_heads_kernel(grad_ref, w_ref, message_ref):
@@ -478,58 +554,110 @@
     )(grad, w_out)
 
 
-def unproject_kernel(
-    landed_ref, query_ref, key_ref, query_gain_ref, key_gain_ref, cosine_ref, sine_ref,
-    grad_ref, gains_ref,
+def tail_kernel(
+    landed_ref, query_ref, key_ref, query_gain_ref, key_gain_ref, cosine_ref, sine_ref, tokens_ref, gain_ref,
+    normed_ref, w_ref, mlp_gain_ref, bias_ref,
+    grad_qkv_ref, input_ref, small_ref, grad_ref, pair_gain_ref, *, every_head,
 ):
-    rows = query_ref.shape[0]
-    half = rows // 2
-
-    @pl.when(pl.program_id(0) == 0)
-    def start():
-        gains_ref[...] = jnp.zeros_like(gains_ref)
-
-    def back(turned, raw_ref, gain_ref, at):
+    double_gains(pair_gain_ref, query_gain_ref, key_gain_ref)
+    rows, width = query_ref.shape
+    depth = tokens_ref.shape[1]
+
+    def back(turned, raw, gain):
         grad = turned * cosine_ref[...] - swap_halves(turned) * sine_ref[...]
-        raw = raw_ref[...]
         scale = lax.rsqrt(head_mean(raw * raw) + EPSILON)
         unit = raw * scale
-        gains_ref[at : at + 1] += jnp.sum(grad * unit, axis=0, keepdims=True)
-        scaled = grad * gain_ref[...]
-        return scale * (scaled - unit * head_mean(scaled * unit))
-
-    key_one = landed_ref[0, :rows].astype(wide)
-    key_two = landed_ref[1, :rows].astype(wide)
-    query_one = landed_ref[0, rows:].astype(wide)
-    query_two = landed_ref[1, rows:].astype(wide)
-    query = jnp.concatenate(
-        [left_pair(query_one, query_two), right_pair(query_one, query_two)], axis=0
+        scaled = grad * gain
+        part = jnp.sum(grad * unit, axis=0, keepdims=True)
+        return (scale * (scaled - unit * head_mean(scaled * unit))).astype(low), part
+
+    query_part = jnp.zeros((1, LANES), wide)
+    key_part = jnp.zeros((1, LANES), wide)
+    for pair in range(width // LANES):
+        span = slice(pair * LANES, (pair + 1) * LANES)
+        key_one = landed_ref[2 * pair, :rows].astype(wide)
+        key_two = landed_ref[2 * pair + 1, :rows].astype(wide)
+        query_one = landed_ref[2 * pair, rows:].astype(wide)
+        query_two = landed_ref[2 * pair + 1, rows:].astype(wide)
+        query = jnp.concatenate(
+            [left_pair(query_one, query_two), right_pair(query_one, query_two)], axis=0
+        )
+        grad_ref[0, :, span], part = back(query, query_ref[:, span], pair_gain_ref[1:2])
+        query_part = query_part + part
+        grad_ref[1, :, span], part = back(
+            left_pair(key_one, key_two), key_ref[:, span], pair_gain_ref[2:3]
+        )
+        key_part = key_part + part
+        grad_ref[2, :, span] = right_pair(key_one, key_two).astype(low)
+    sums = dot_nt(grad_ref[0], w_ref[0]) + dot_nt(grad_ref[1], w_ref[1])
+    sums = sums + dot_nt(grad_ref[2], w_ref[2])
+    x = tokens_ref[...].astype(wide)
+    scale = lax.rsqrt(jnp.mean(x * x, axis=1, keepdims=True) + EPSILON)
+    unit = x * scale
+    gain_part = jnp.sum(sums * unit, axis=0, keepdims=True)
+    scaled = sums * gain_ref[...]
+    part = scale * (scaled - unit * jnp.mean(scaled * unit, axis=1, keepdims=True))
+    input_ref[...] = part.astype(low)
+    for index in range(3):
+        grad_qkv_ref[index] = dot_nn(normed_ref[...], grad_ref[index]).astype(low)
+    count = depth // LANES
+    small_ref[...] = jnp.zeros_like(small_ref)
+    for row in range(count):
+        small_ref[row : row + 1, :] = gain_part[:, row * LANES : (row + 1) * LANES]
+    small_ref[count : 2 * count, :] = mlp_gain_ref[...]
+    small_ref[2 * count : 2 * count + 1, :] = query_part
+    small_ref[2 * count + 1 : 2 * count + 2, :] = key_part
+    head = lax.axis_index("tensor") * (width // HD) + lax.axis_index("dp") // every_head
+    lane = lax.broadcasted_iota(jnp.int32, (1, LANES), 1)
+    for row in range(2):
+        total = jnp.sum(bias_ref[row], keepdims=True)
+        at = 2 * count + 2 + row
+        small_ref[at : at + 1, :] = jnp.where(lane == head, total, 0.0)
+
+
+def tail(
+    landed, raw_query, raw_key, query_gain, key_gain, cosine, sine, tokens, gain, normed_turned,
+    w_qkv, mlp_gain_part, bias_tiles, ranks,
+):
+    rows, width = raw_query.shape
+    depth = tokens.shape[1]
+    small = -(-(2 * depth // LANES + 4) // 8) * 8
+    return pl.pallas_call(
+        functools.partial(tail_kernel, every_head=ranks),
+        in_specs=[WHOLE] * 13,
+        out_specs=(WHOLE,) * 3,
+        out_shape=(
+            jax.ShapeDtypeStruct((3, depth, width), low),
+            jax.ShapeDtypeStruct((rows, depth), low),
+            jax.ShapeDtypeStruct((small, LANES), wide),
+        ),
+        scratch_shapes=[pltpu.VMEM((3, rows, width), low), pltpu.VMEM((8, LANES), wide)],
+        compiler_params=params(),
+    )(
+        landed, raw_query, raw_key, query_gain, key_gain, cosine, sine, tokens, gain, normed_turned,
+        w_qkv, mlp_gain_part, bias_tiles,
     )
-    grad_ref[0] = back(query, query_ref, query_gain_ref, 0).astype(low)
-    grad_ref[1] = back(left_pair(key_one, key_two), key_ref, key_gain_ref, 1).astype(low)
-    grad_ref[2] = right_pair(key_one, key_two).astype(low)
-
-
-def unproject(landed, raw_query, raw_key, query_gain, key_gain, cosine, sine):
-    rows, width = raw_query.shape
-    column = pl.BlockSpec((rows, LANES), lambda i: (0, i))
+
+
+def widen_kernel(*refs):
+    half = len(refs) // 2
+    for source, target in zip(refs[:half], refs[half:]):
+        target[...] = source[...].astype(wide)
+
+
+def widen(arrays):
+    steps = 8
+    while any(a.shape[0] % (16 * steps) for a in arrays):
+        steps //= 2
+    specs = [pl.BlockSpec((a.shape[0] // steps, a.shape[1]), lambda i: (i, 0)) for a in arrays]
     return pl.pallas_call(
-        unproject_kernel,
-        grid=(width // LANES,),
-        in_specs=[
-            pl.BlockSpec((2, rows + rows // 2, LANES), lambda i: (i, 0, 0)),
-            column, column, WHOLE, WHOLE, WHOLE, WHOLE,
-        ],
-        out_specs=(
-            pl.BlockSpec((3, rows, LANES), lambda i: (0, 0, i)),
-            pl.BlockSpec((8, LANES), lambda i: (0, 0)),
-        ),
-        out_shape=(
-            jax.ShapeDtypeStruct((3, rows, width), low),
-            jax.ShapeDtypeStruct((8, LANES), wide),
-        ),
+        widen_kernel,
+        grid=(steps,),
+        in_specs=specs,
+        out_specs=tuple(specs),
+        out_shape=tuple(jax.ShapeDtypeStruct(a.shape, wide) for a in arrays),
         compiler_params=params(),
-    )(landed, raw_query, raw_key, query_gain, key_gain, cosine, sine)
+    )(*arrays)
 
 
 def remote(src, dst, send, recv, place):
@@ -539,8 +667,11 @@
     )
 
 
-def greet(heads, ranks, head, rank, with_ranks):
+def greet(heads, ranks, head, rank, with_ranks, tensor=1):
     barrier = pltpu.get_barrier_semaphore()
+    for step in range(1, tensor):
+        side = lax.rem(lax.axis_index("tensor") + step, tensor)
+        pl.semaphore_signal(barrier, inc=1, device_id={"tensor": side}, device_id_type=MESH)
     for step in range(1, heads):
         place = lax.rem(head + step, heads) * ranks + rank
         pl.semaphore_signal(barrier, inc=1, device_id={"dp": place}, device_id_type=MESH)
@@ -548,19 +679,31 @@
         for step in range(1, ranks):
             place = head * ranks + lax.rem(rank + step, ranks)
             pl.semaphore_signal(barrier, inc=1, device_id={"dp": place}, device_id_type=MESH)
-    pl.semaphore_wait(barrier, heads - 1 + (ranks - 1 if with_ranks else 0))
+    pl.semaphore_wait(barrier, heads + tensor - 2 + (ranks - 1 if with_ranks else 0))
 
 
 def spread_kernel(
-    message_ref, kv_ref, query_ref, send_a, recv_a, send_b, recv_b, send_f, recv_f, local, *, ranks
+    message_ref, w_ref, kv_ref, query_ref, others_ref,
+    send_a, recv_a, send_b, recv_b, send_f, recv_f, send_w, recv_w, local, *, ranks
 ):
     heads = message_ref.shape[0]
+    tensor = others_ref.shape[0] + 1
+    side = lax.axis_index("tensor")
     size = kv_ref.shape[2]
     rest = query_ref.shape[1]
     place = lax.axis_index("dp")
     head = place // ranks
     rank = lax.rem(place, ranks)
-    greet(heads, ranks, head, rank, True)
+    greet(heads, ranks, head, rank, True, tensor)
+    onward = []
+    for step in range(1, tensor):
+        copy = pltpu.make_async_remote_copy(
+            src_ref=w_ref, dst_ref=others_ref.at[tensor - step - 1],
+            send_sem=send_w.at[step], recv_sem=recv_w.at[step],
+            device_id={"tensor": lax.rem(side + step, tensor)}, device_id_type=MESH,
+        )
+        copy.start()
+        onward.append(copy)
     firsts = []
     for step in range(1, heads):
         to = lax.rem(head + step, heads)
@@ -582,7 +725,6 @@
     ]
     for copy in mine:
         copy.start()
-    onward = []
 
     def forward(step, source, src):
         for other in range(1, ranks):
@@ -605,28 +747,50 @@
         copy.wait()
 
 
-def spread(message, ranks, rows):
+def spread(message, w_out, ranks, rows, tensor):
     heads, size = message.shape[:2]
     dma = pltpu.SemaphoreType.DMA
     return pl.pallas_call(
         functools.partial(spread_kernel, ranks=ranks),
-        in_specs=[ANYWHERE],
-        out_specs=(ANYWHERE, ANYWHERE),
+        in_specs=[ANYWHERE] * 2,
+        out_specs=(ANYWHERE,) * 3,
         out_shape=(
             jax.ShapeDtypeStruct((ranks, heads, rows + IDS, LANES), low),
             jax.ShapeDtypeStruct((heads, rows // 2, LANES), low),
+            jax.ShapeDtypeStruct((tensor - 1,) + w_out.shape, low),
         ),
-        scratch_shapes=[dma((heads,))] * 4 + [dma((heads, ranks))] * 2 + [dma((2,))],
+        scratch_shapes=[dma((heads,))] * 4 + [dma((heads, ranks))] * 2 + [dma((tensor,))] * 2 + [dma((2,))],
         compiler_params=params(collective_id=0, has_side_effects=True),
-    )(message)
-
-
-def exchange_kernel(message_ref, landed_ref, send, recv, local, *, ranks):
+    )(message, w_out)
+
+
+def send_shares(part_ref, shares_ref, send, recv):
+    tensor, _, share = shares_ref.shape
+    tensor += 1
+    side = lax.axis_index("tensor")
+    copies = []
+    for step in range(1, tensor):
+        to = lax.rem(side + step, tensor)
+        copies.append(
+            pltpu.make_async_remote_copy(
+                src_ref=part_ref.at[:, pl.ds(pl.multiple_of(to * share, LANES), share)],
+                dst_ref=shares_ref.at[tensor - step - 1],
+                send_sem=send.at[step], recv_sem=recv.at[step],
+                device_id={"tensor": to}, device_id_type=MESH,
+            )
+        )
+        copies[-1].start()
+    return copies
+
+
+def exchange_kernel(
+    message_ref, part_ref, landed_ref, shares_ref, send, recv, send_t, recv_t, local, *, ranks
+):
     heads = message_ref.shape[0]
     place = lax.axis_index("dp")
     head = place // ranks
     rank = lax.rem(place, ranks)
-    greet(heads, ranks, head, rank, False)
+    greet(heads, ranks, head, rank, False, shares_ref.shape[0] + 1)
     copies = []
     for step in range(1, heads):
         to = lax.rem(head + step, heads)
@@ -639,21 +803,26 @@
         copies[-1].start()
     copies.append(pltpu.make_async_copy(message_ref.at[head], landed_ref.at[head], local))
     copies[-1].start()
+    copies += send_shares(part_ref, shares_ref, send_t, recv_t)
     for copy in copies:
         copy.wait()
 
 
-def exchange(message, ranks, collective_id):
+def exchange(message, part, ranks, tensor):
     heads = message.shape[0]
+    rows, depth = part.shape
     dma = pltpu.SemaphoreType.DMA
     return pl.pallas_call(
         functools.partial(exchange_kernel, ranks=ranks),
-        in_specs=[ANYWHERE],
-        out_specs=ANYWHERE,
-        out_shape=jax.ShapeDtypeStruct(message.shape, message.dtype),
-        scratch_shapes=[dma((heads,)), dma((heads,)), dma],
-        compiler_params=params(collective_id=collective_id, has_side_effects=True),
-    )(message)
+        in_specs=[ANYWHERE] * 2,
+        out_specs=(ANYWHERE,) * 2,
+        out_shape=(
+            jax.ShapeDtypeStruct(message.shape, message.dtype),
+            jax.ShapeDtypeStruct((tensor - 1, rows, depth // tensor), low),
+        ),
+        scratch_shapes=[dma((heads,))] * 2 + [dma((tensor,))] * 2 + [dma],
+        compiler_params=params(collective_id=2, has_side_effects=True),
+    )(message, part)
 
 
 def share_out_kernel(message_ref, landed_ref, send, recv, send_t, recv_t, local, *, ranks, tensor):
@@ -720,11 +889,11 @@
 
 
 def total_kernel(*refs, arrays, chunks, zs, tensor):
-    ins, refs = refs[: arrays + 1], refs[arrays + 1 :]
-    outs, refs = refs[: arrays + 1], refs[arrays + 1 :]
+    ins, part_ref, refs = refs[: arrays + 1], refs[arrays + 1], refs[arrays + 2 :]
+    outs, shares_ref, refs = refs[: arrays + 1], refs[arrays + 1], refs[arrays + 2 :]
     count = len(chunks)
     scratch, refs = refs[: 5 * count], refs[5 * count :]
-    near_ref, far_ref, line_ref, side_ref, send, recv, send_z, recv_z, send_s, recv_s = refs
+    near_ref, far_ref, line_ref, side_ref, send, recv, send_z, recv_z, send_s, recv_s, send_t, recv_t = refs
     place = lax.axis_index("dp")
     side = lax.axis_index("tensor")
     core = lax.rem(place, 2)
@@ -742,6 +911,7 @@
         to = lax.rem(side + step, tensor)
         pl.semaphore_signal(barrier, inc=1, device_id={"tensor": to}, device_id_type=MESH)
     pl.semaphore_wait(barrier, zs + tensor)
+    shares = send_shares(part_ref, shares_ref, send_t, recv_t)
     sent = []
     waits = {}
 
@@ -896,9 +1066,11 @@
         arrived((chunk, 5))
     for copy in sent:
         copy.wait_send()
-
-
-def total_sums(arrays, small, dp, tensor):
+    for copy in shares:
+        copy.wait()
+
+
+def total_sums(arrays, small, part, dp, tensor):
     zs = dp // 4
     chunks = []
     scratch = []
@@ -921,9 +1093,10 @@
         functools.partial(
             total_kernel, arrays=len(arrays), chunks=tuple(chunks), zs=zs, tensor=tensor
         ),
-        in_specs=[WHOLE] * (len(arrays) + 1),
-        out_specs=(WHOLE,) * (len(arrays) + 1),
-        out_shape=tuple(jax.ShapeDtypeStruct(a.shape, a.dtype) for a in [*arrays, small]),
+        in_specs=[WHOLE] * (len(arrays) + 1) + [ANYWHERE],
+        out_specs=(WHOLE,) * (len(arrays) + 1) + (ANYWHERE,),
+        out_shape=tuple(jax.ShapeDtypeStruct(a.shape, a.dtype) for a in [*arrays, small])
+        + (jax.ShapeDtypeStruct((tensor - 1, part.shape[0], part.shape[1] // tensor), low),),
         scratch_shapes=scratch
         + [
             pltpu.VMEM((2,) + small.shape, wide),
@@ -933,9 +1106,10 @@
         ]
         + [dma((count, 4))] * 2
         + [dma((count, 2, zs))] * 2
-        + [dma((4, max(zs, tensor)))] * 2,
+        + [dma((4, max(zs, tensor)))] * 2
+        + [dma((tensor,))] * 2,
         compiler_params=params(collective_id=4, has_side_effects=True),
-    )(*arrays, small)
+    )(*arrays, small, part)
 
 
 def collect_kernel(
@@ -1061,7 +1235,6 @@
     tensor = lax.axis_size("tensor")
     ranks = dp // heads
     place = lax.axis_index("dp")
-    head_here = place // ranks
     rank_here = lax.rem(place, ranks)
     width_share = tokens.shape[1] // tensor
     tensor_start = lax.axis_index("tensor") * width_share
@@ -1071,115 +1244,72 @@
             return x + lax.ppermute(x_low, "tensor", [(0, 1), (1, 0)]).astype(wide)
         return lax.psum(x_low, "tensor").astype(wide)
 
-    def tensor_share(x):
-        mine = lax.dynamic_slice_in_dim(x, tensor_start, width_share, 1)
-        if tensor == 2:
-            other = lax.dynamic_slice_in_dim(x, width_share - tensor_start, width_share, 1)
-            return mine + lax.ppermute(other.astype(low), "tensor", [(0, 1), (1, 0)]).astype(wide)
-        return lax.psum_scatter(x, "tensor", scatter_dimension=1, tiled=True)
-
+    def share_of(x):
+        return lax.dynamic_slice_in_dim(x, tensor_start, width_share, 1).astype(wide)
+
+    def share_sum(x, others):
+        return share_of(x) + jnp.sum(others.astype(wide), axis=0)
+
+    depth = tokens.shape[1]
     cosine, sine = tables(time)
-    pair_gain = lambda gain: jnp.concatenate([gain, gain])[None, :]
-    ids = jnp.concatenate([id_rows(segment), id_rows(variate)])
-    w_outs = [w_out] + [
-        lax.ppermute(w_out, "tensor", [((i + step) % tensor, i) for i in range(tensor)])
-        for step in range(1, tensor)
-    ]
     message, raw_query, raw_key, normed_one = project(
-        tokens, w_qkv, attn_gain[None, :], pair_gain(query_gain * (LOG2E * HD**-0.5)),
-        pair_gain(key_gain), cosine, sine, ids,
+        tokens, w_qkv, attn_gain[None, :], query_gain[None, :], key_gain[None, :], cosine, sine,
+        segment.reshape(-1, LANES), variate.reshape(-1, LANES),
     )
-    kv, query_in = spread(message, ranks, rows)
-    key_op, value_op, query_op, exact, out_message, runs = forward_attention(
-        var_bias, kv, query_in
+    kv, query_in, w_others = spread(message, w_out, ranks, rows, tensor)
+    key_op, value_op, query_op, exact, out_message, runs = forward_attention(var_bias, kv, query_in)
+    landed = share_out(out_message, ranks, tensor)
+    heads_out, middle, normed_two, hidden, grad_gu, middle_part, middle_low, mlp_gain_part = out_and_mlp(
+        landed, tokens, cotangent, mlp_gain[None, :], w_out, w_others, w_gateup, w_down
     )
-    heads_out, attn_total = attention_out(share_out(out_message, ranks, tensor), w_outs)
-    inputs = tokens.astype(wide)
-    middle = inputs + attn_total
-    scale_two = lax.rsqrt(jnp.mean(middle * middle, axis=1, keepdims=True) + EPSILON)
-    unit_two = middle * scale_two
-    normed_two = (unit_two * mlp_gain).astype(low)
-    gate_up = jnp.einsum("td,kdf->ktf", normed_two, w_gateup, preferred_element_type=wide)
-    gate_vals = gate_up[0]
-    up_vals = gate_up[1]
-    sig_gate = jax.nn.sigmoid(gate_vals)
-    act_gate = gate_vals * sig_gate
-    hidden = (act_gate * up_vals).astype(low)
-    mlp_part = jnp.dot(hidden, w_down, preferred_element_type=wide)
-    grad_hidden = jnp.einsum("te,fe->tf", cotangent, w_down, preferred_element_type=wide)
-    grad_gate = grad_hidden * up_vals * sig_gate * (1.0 + gate_vals * (1.0 - sig_gate))
-    grad_up = grad_hidden * act_gate
-    grad_gu = jnp.stack([grad_gate, grad_up]).astype(low)
-    grad_normed_two = jnp.einsum("ktf,kdf->td", grad_gu, w_gateup, preferred_element_type=wide)
-    mlp_gain_part = jnp.sum(grad_normed_two * unit_two, axis=0)
-    scaled_two = grad_normed_two * mlp_gain
-    middle_part = scale_two * (
-        scaled_two - unit_two * jnp.mean(scaled_two * unit_two, axis=1, keepdims=True)
-    )
-    middle_low, hidden_late, grad_gu_late = lax.optimization_barrier(
-        (middle_part.astype(low), hidden, grad_gu)
-    )
-    grad_down = jnp.einsum("tf,te->fe", hidden_late, cotangent, preferred_element_type=wide)
-    grad_gateup = jnp.einsum("td,ktf->kdf", normed_two, grad_gu_late, preferred_element_type=wide)
+    grad_down = jnp.einsum("tf,te->fe", hidden, cotangent, preferred_element_type=wide)
+    grad_gateup = jnp.einsum("td,ktf->kdf", normed_two, grad_gu, preferred_element_type=wide)
     early = (keep_order(grad_gateup.astype(low)), grad_down.astype(low))
+    mlp_part = jnp.dot(hidden, w_down, preferred_element_type=wide).astype(low)
+    normed_turned = normed_one.T
     grad_middle = cotangent.astype(wide) + tensor_sum(middle_part, middle_low)
     grad_middle_low = grad_middle.astype(low)
-    grad_middle_low, mlp_part = lax.optimization_barrier((grad_middle_low, mlp_part))
-    mlp_share = tensor_share(mlp_part)
-    output = (lax.dynamic_slice_in_dim(middle, tensor_start, width_share, 1) + mlp_share).astype(low)
+    grad_middle_low, mlp_part, normed_turned = lax.optimization_barrier(
+        (grad_middle_low, mlp_part, normed_turned)
+    )
     grad_out = jnp.einsum("tc,td->cd", heads_out, grad_middle_low, preferred_element_type=wide)
     early = lax.psum((*early, grad_out.astype(low)), "dp")
-    grad_landed = exchange(grad_heads_of(grad_middle_low, w_out), ranks, 2)
+    out_sum = early[2]
+    grad_landed, mlp_others = exchange(
+        grad_heads_of(grad_middle_low, w_out), mlp_part, ranks, tensor
+    )
+    output = (share_of(middle) + share_sum(mlp_part, mlp_others)).astype(low)
     own_ids = lax.dynamic_index_in_dim(kv[:, :, rows:], rank_here, 0, False)
     back_kv, back_query, bias_tiles = backward_attention(
         runs, key_op, value_op, query_op, exact, grad_landed, own_ids
     )
-    same_sum = jnp.sum(bias_tiles[0])
-    other_sum = jnp.sum(bias_tiles[1])
-    grad_projected, gain_tile = unproject(
-        collect(back_kv, back_query), raw_query, raw_key, pair_gain(query_gain),
-        pair_gain(key_gain), cosine, sine,
+    grad_qkv, input_part, small = tail(
+        collect(back_kv, back_query), raw_query, raw_key, query_gain[None, :], key_gain[None, :],
+        cosine, sine, tokens, attn_gain[None, :], normed_turned, w_qkv, mlp_gain_part, bias_tiles, ranks,
     )
-    query_gain_part = gain_tile[0, :HD] + gain_tile[0, HD:]
-    key_gain_part = gain_tile[1, :HD] + gain_tile[1, HD:]
-    scale_one = lax.rsqrt(jnp.mean(inputs * inputs, axis=1, keepdims=True) + EPSILON)
-    unit_one = inputs * scale_one
-    grad_qkv = jnp.einsum("td,kte->kde", normed_one, grad_projected, preferred_element_type=wide)
-    grad_normed_one = jnp.einsum("kte,kde->td", grad_projected, w_qkv, preferred_element_type=wide)
-    attn_gain_part = jnp.sum(grad_normed_one * unit_one, axis=0)
-    scaled_one = grad_normed_one * attn_gain
-    input_part = scale_one * (
-        scaled_one - unit_one * jnp.mean(scaled_one * unit_one, axis=1, keepdims=True)
+    qkv_sum, small, input_others = total_sums([grad_qkv], small, input_part, dp, tensor)
+    grad_input = share_of(grad_middle) + share_sum(input_part, input_others)
+    flat = lambda x: x.reshape(-1, x.shape[-1])
+    qkv_wide, out_wide, gateup_wide, down_wide = widen(
+        [flat(qkv_sum), out_sum, flat(early[0]), early[1]]
     )
-    grad_input = lax.dynamic_slice_in_dim(grad_middle, tensor_start, width_share, 1) + tensor_share(
-        input_part
-    )
-    depth = tokens.shape[1]
-    head_slot = lax.axis_index("tensor") * heads + head_here
-    hit = (jnp.arange(tensor * heads, dtype=jnp.int32) == head_slot).astype(wide)
-    small = jnp.concatenate(
-        [attn_gain_part, mlp_gain_part, query_gain_part, key_gain_part]
-        + [same_sum * hit, other_sum * hit]
-    )
-    length = small.shape[0]
-    small = jnp.pad(small, (0, -length % (8 * LANES))).reshape(-1, LANES)
-    qkv_sum, small = total_sums([grad_qkv.astype(low)], small, dp, tensor)
-    small = small.reshape(-1)[:length]
-    gains, biases = small[: 2 * depth + 2 * HD], small[2 * depth + 2 * HD :]
+    count = 2 * depth // LANES
+    gains = small[:count].reshape(2, depth)
+    head_gains = small[count : count + 2, :HD] + small[count : count + 2, HD:]
     bias_sum = lax.dynamic_slice_in_dim(
-        biases.reshape(2, tensor * heads), lax.axis_index("tensor") * heads, heads, 1
+        small[count + 2 : count + 4], lax.axis_index("tensor") * heads, heads, 1
     )
     return (
         output,
         grad_input,
-        qkv_sum.astype(wide),
-        early[2].astype(wide),
-        early[0].astype(wide),
-        early[1].astype(wide),
-        gains[:depth],
-        gains[depth : 2 * depth],
-        gains[2 * depth : 2 * depth + HD],
-        gains[2 * depth + HD :],
+        qkv_wide.reshape(w_qkv.shape),
+        out_wide,
+        gateup_wide.reshape(w_gateup.shape),
+        down_wide,
+        gains[0],
+        gains[1],
+        head_gains[0],
+        head_gains[1],
         bias_sum,
     )
 

time: 462 us -> 443 us (0.959)
  Pallas kernels: 340 us -> 376 us
  other arithmetic: 38.6 us -> 9.04 us
  matrix products: 36.3 us -> 16 us
    pallas_call x2 -> x3, Pallas kernels: 10.9 us -> 44.8 us  [the longest x1 18 us: out_and_mlp(): pl.pallas_call(mlp_kernel, in_specs=[WHOLE] * 6 + [ANYWHERE] * 2, out_spe...]
    convert_element_type x7 -> x0, other arithmetic: 22.9 us -> none  [the longest x1 7.96 us: shards(): early[0].astype(wide)]
    dot_general x8 -> x3, matrix products: 34.6 us -> 14.3 us  [the longest x1 5.12 us: shards(): jnp.einsum('td,ktf->kdf', normed_two, grad_gu, preferred_element_type=wide)]
    pallas_call x1, Pallas kernels: 67.8 us -> 73.4 us  [backward_attention(): pl.pallas_call(backward_kernel, grid_spec=pltpu.PrefetchScalarGridSpec(nu...]
    ppermute x1, waiting for transfers between devices: 12.2 us -> 6.71 us  [tensor_sum(): return x + lax.ppermute(x_low, 'tensor', [(0, 1), (1, 0)]).astype(wide)]
  transfers between devices with their start and end apart: 5 -> 2, of which waited for: 1 -> 2; matrix products, arithmetic and copies ran while one was open for 11% -> 6% of each run, Pallas kernels for 74% -> 54%
where the time goes in v1:
time: 443 us; the launch traced here: 435 us
  Pallas kernels  376 us (85%)
  matrix products  16 us (4%)
  between operations  14.7 us (3%)
  waiting for transfers between devices  10.6 us (2%)
  other arithmetic  9.04 us (2%)
  local copies, waits for them, and re-layouts  7.98 us (2%)
    pallas_call x1, Pallas kernels, total_sums(): pl.pallas_call(functools.partial(total_kernel, arrays=len(arrays), chunks...  76.3 us
    pallas_call x1, Pallas kernels, backward_attention(): pl.pallas_call(backward_kernel, grid_spec=pltpu.PrefetchScalarGridSpec(nu...  73.4 us
    pallas_call x1, Pallas kernels, collect(): pl.pallas_call(functools.partial(collect_kernel, ranks=ranks), in_specs=[...  53.1 us
    pallas_call x1, Pallas kernels, forward_attention(): pl.pallas_call(forward_kernel, grid=(heads,), in_specs=[SCALARS, WHOLE, f...  40 us
    pallas_call x1, Pallas kernels, spread(): pl.pallas_call(functools.partial(spread_kernel, ranks=ranks), in_specs=[A...  38.9 us
    pallas_call x1, Pallas kernels, share_out(): pl.pallas_call(functools.partial(share_out_kernel, ranks=ranks, tensor=te...  20.5 us
    pallas_call x1, Pallas kernels, out_and_mlp(): pl.pallas_call(mlp_kernel, in_specs=[WHOLE] * 6 + [ANYWHERE] * 2, out_spe...  18 us
    pallas_call x1, Pallas kernels, exchange(): pl.pallas_call(functools.partial(exchange_kernel, ranks=ranks), in_specs=...  17.8 us
  transfers between devices with their start and end apart: 2, of which 2 were waited for; matrix products, arithmetic and copies ran while one was open for 6% of the time, Pallas kernels for 54%

profile of v1, /device:TPU:8, one launch (start us, length us, event | category | flops | bytes accessed | tf_op | source)
XLA Modules:
  0.0 434.6 jit_solution(17819242150695191125)
XLA Ops:
  7.2 0.0 all-reduce.3.cloned.1.call-start
  7.2 0.7 convert_element_type.38
  7.9 2.5 fusion.4
  10.4 7.4 %shard_map.239 = (bf16[8,784,128]{2,1,0:T(8,128)(2,1)}, f32[512,512]{1,0:T(8,128)}, f32[512,512]{1,0:T(8,128)}, bf16[512,1024]{1,0:T(8,128)(2,1)}) custom-call(bf16[512,1024]{1,0:T(8,128)(2,1)} %tokens_ref.5, bf16[3,1024,512]{2,1,0:T(8,128)(2,1)} %w_ref.7, f32[1,1024]{1,0:T(1,128)} %bitcast.42, f32[1,64]{1,0:T(1,128)} %bitcast.47, f32[1,64]{1,0:T(1,128)} %bitcast.49, ...), custom_call_target="tpu_custom_call" | custom-call | tf_op jit(solution)/shard_map/pallas_call | solution.py:188
  17.8 38.9 %shard_map.240 = (bf16[2,8,528,128]{3,2,1,0:T(8,128)(2,1)}, bf16[8,256,128]{2,1,0:T(8,128)(2,1)}, bf16[1,512,1024]{2,1,0:T(8,128)(2,1)}) custom-call(bf16[8,784,128]{2,1,0:T(8,128)(2,1)} %get-tuple-element.50.message_ref, bf16[512,1024]{1,0:T(8,128)(2,1)} %w_ref.6), custom_call_target="tpu_custom_call" | custom-call | tf_op jit(solution)/shard_map/pallas_call | solution.py:753
  56.7 40.0 %shard_map.241 = (bf16[8192,128]{1,0:T(8,128)(2,1)}, bf16[8192,128]{1,0:T(8,128)(2,1)}, bf16[4096,128]{1,0:T(8,128)(2,1)}, f32[4096,128]{1,0:T(8,128)}, bf16[8,256,128]{2,1,0:T(8,128)(2,1)}, /*index=5*/s32[2,16]{1,0:T(2,128)}) custom-call(f32[2,8]{1,0:T(2,128)} %bias_ref.1, bf16[2,8,528,128]{3,2,1,0:T(8,128)(2,1)} %get-tuple-element.51.kv_ref, ...), custom_call_target="tpu_custom_call" | custom-call | tf_op jit(solution)/shard_map/pallas_call | solution.py:313
  96.7 20.5 %shard_map.242.landed_ref = bf16[2,8,256,128]{3,2,1,0:T(8,128)(2,1)} custom-call(bf16[8,256,128]{2,1,0:T(8,128)(2,1)} %get-tuple-element.53.message_ref), custom_call_target="tpu_custom_call" | custom-call | tf_op jit(solution)/shard_map/pallas_call | solution.py:881
  117.2 0.0 copy-start.2
  117.3 18.0 %shard_map.243 = (bf16[512,512]{1,0:T(8,128)(2,1)}, f32[512,1024]{1,0:T(8,128)}, bf16[512,1024]{1,0:T(8,128)(2,1)}, bf16[512,1408]{1,0:T(8,128)(2,1)}, bf16[2,51...) custom-call(bf16[2,8,256,128]{3,2,1,0:T(8,128)(2,1)} %shard_map.242.landed_ref, ...), custom_call_target="tpu_custom_call" | custom-call | tf_op jit(solution)/shard_map/pallas_call | solution.py:514
  135.2 0.6 collective-permute-start
  135.8 0.0 copy-done.2
  135.8 4.3 %convolution_convert_fusion.2.part_ref = bf16[512,1024]{1,0:T(8,128)(2,1)} fusion(bf16[512,1408]{1,0:T(8,128)(2,1)} %get-tuple-element.58, bf16[1408,1024]{1,0:T(8,128)(2,1)S(1)} %copy-done.2), kind=kOutput, calls=%fused_computation.3 | convolution fusion | flops 1476919296 | bytes 5373952 | tf_op jit(solution)/shard_map/dot_general | solution.py:1268
  140.1 0.0 copy-start
  140.1 2.4 copy.27
  142.5 0.0 copy-done
  142.5 0.0 copy-start.6
  142.5 0.0 copy-start.7
  142.5 4.8 %convolution_convert_fusion.1 = bf16[1408,1024]{1,0:T(8,128)(2,1)} fusion(bf16[512,1408]{1,0:T(8,128)(2,1)} %get-tuple-element.58, bf16[512,1024]{1,0:T(8,128)(2,1)S(1)} %copy-done), kind=kOutput, calls=%fused_computation.1 | convolution fusion | flops 1477836800 | bytes 5373952 | tf_op jit(solution)/shard_map/tf,te->fe/dot_general | solution.py:1265
  147.3 0.0 copy-done.6
  147.3 0.0 copy-done.7
  147.3 0.0 copy-start.4
  147.3 5.1 %convolution_convert_fusion = bf16[2,1408,1024]{1,2,0:T(8,128)(2,1)} fusion(bf16[2,512,1408]{2,1,0:T(8,128)(2,1)S(1)} %copy-done.6, bf16[512,1024]{1,0:T(8,128)(2,1)S(1)} %copy-done.7), kind=kOutput, calls=%fused_computation | convolution fusion | flops 2955673600 | bytes 9699328 | tf_op jit(solution)/shard_map/td,ktf->kdf/dot_general | solution.py:1266
  152.4 6.7 %collective-permute-done = bf16[512,1024]{1,0:T(8,128)(2,1)} collective-permute-done((bf16[512,1024]{1,0:T(8,128)(2,1)}, bf16[512,1024]{1,0:T(8,128)(2,1)}, u32[]{:S(2)}, u32[]{:S(2)}) %collective-permute-start) | collective-permute-done | bytes 1048608 | tf_op jit(solution)/shard_map/ppermute | solution.py:1244
  159.1 0.0 copy-done.4
  159.1 0.0 copy-start.8
  159.1 1.9 fusion.5
  161.0 0.0 copy-start.1
  161.0 1.0 copy-done.1
  162.0 0.0 copy-done.8
  162.0 1.7 convolution_convert_fusion.3
  163.8 0.0 all-reduce.3.cloned.1.call-update
  163.8 0.9 slice.29
  164.7 0.6 dynamic-slice_bitcast_fusion.ids_ref
  165.3 3.7 shard_map.244.message_ref
  168.9 17.8 %shard_map.245 = (bf16[8,256,128]{2,1,0:T(8,128)(2,1)}, bf16[1,512,512]{2,1,0:T(8,128)(2,1)}) custom-call(bf16[8,256,128]{2,1,0:T(8,128)(2,1)} %shard_map.244.message_ref, bf16[512,1024]{1,0:T(8,128)(2,1)} %convolution_convert_fusion.2.part_ref), custom_call_target="tpu_custom_call" | custom-call | tf_op jit(solution)/shard_map/pallas_call | solution.py:815
  186.8 73.4 %shard_map.246 = (bf16[2,8,512,128]{3,2,1,0:T(8,128)(2,1)}, bf16[8,256,128]{2,1,0:T(8,128)(2,1)}, f32[2,8,128]{2,1,0:T(8,128)}) custom-call(s32[2,16]{1,0:T(2,128)} %get-tuple-element.63.runs_ref, bf16[8192,128]{1,0:T(8,128)(2,1)} %get-tuple-element.64.k_ref, bf16[8192,128]{1,0:T(8,128)(2,1)} %get-tuple-element.65.v_ref, ...), custom_call_target="tpu_custom_call" | custom-call | tf_op jit(solution)/shard_map/pallas_call | solution.py:414
  260.1 53.1 %shard_map.247.landed_ref = bf16[8,768,128]{2,1,0:T(8,128)(2,1)} custom-call(bf16[2,8,512,128]{3,2,1,0:T(8,128)(2,1)} %get-tuple-element.69.kv_ref, bf16[8,256,128]{2,1,0:T(8,128)(2,1)} %get-tuple-element.70.query_ref), custom_call_target="tpu_custom_call" | custom-call | tf_op jit(solution)/shard_map/pallas_call | solution.py:1181
  313.2 12.6 %shard_map.248 = (bf16[3,1024,512]{2,1,0:T(8,128)(2,1)}, bf16[512,1024]{1,0:T(8,128)(2,1)}, f32[24,128]{1,0:T(8,128)}) custom-call(bf16[8,768,128]{2,1,0:T(8,128)(2,1)} %shard_map.247.landed_ref, f32[512,512]{1,0:T(8,128)} %get-tuple-element.71.query_ref, f32[512,512]{1,0:T(8,128)} %get-tuple-element.72.key_ref, f32[1,64]{1,0:T(1,128)} %bitcast.48, ...), custom_call_target="tpu_custom_call" | custom-call | tf_op jit(solution)/shard_map/pallas_call | solution.py:625
  325.8 0.0 copy-start.3
  325.8 0.0 copy-start.5
  325.8 76.3 %shard_map.249 = (bf16[3,1024,512]{2,1,0:T(8,128)(2,1)}, f32[24,128]{1,0:T(8,128)}, bf16[1,512,512]{2,1,0:T(8,128)(2,1)}) custom-call(bf16[3,1024,512]{2,1,0:T(8,128)(2,1)} %get-tuple-element.77.refs_0_, f32[24,128]{1,0:T(8,128)} %get-tuple-element.78.refs_1_, bf16[512,1024]{1,0:T(8,128)(2,1)} %get-tuple-element.76.refs_2_), custom_call_target="tpu_custom_call" | custom-call | tf_op jit(solution)/shard_map/pallas_call | solution.py:1092
  402.1 0.7 slice.36
  402.8 0.6 constant_dynamic-slice_fusion
  403.4 0.8 slice_add_fusion
  404.2 0.5 slice_bitcast_fusion.2
  404.7 1.3 slice_bitcast_fusion
  406.0 0.0 copy-done.3
  406.0 0.0 copy-done.5
  406.0 3.1 fusion
  409.1 3.8 all-reduce.3.cloned.1.call-done
  413.0 14.3 %shard_map.250 = (f32[3072,512]{1,0:T(8,128)}, f32[512,1024]{1,0:T(8,128)}, f32[2048,1408]{1,0:T(8,128)}, f32[1408,1024]{1,0:T(8,128)}) custom-call(bf16[3072,512]{1,0:T(8,128)(2,1)} %bitcast.41, bf16[512,1024]{1,0:T(8,128)(2,1)} %get-tuple-element.89.refs_1_, bf16[2048,1408]{1,0:T(8,128)(2,1)} %get-tuple-element.90.refs_2_, ...), custom_call_target="tpu_custom_call" | custom-call | tf_op jit(solution)/shard_map/pallas_call | solution.py:653
Async XLA Ops:
  7.2 405.8 %all-reduce.3.cloned.1.call-start = ((), (), s32[]{:S(2)}) async-start(), calls=%async_computation | async-start | bytes 19398656 | tf_op jit(solution)/shard_map/psum | solution.py:1276
  117.2 18.5 %copy-start.2 = (bf16[1408,1024]{1,0:T(8,128)(2,1)S(1)}, bf16[1408,1024]{1,0:T(8,128)(2,1)}, u32[]{:S(2)}) copy-start(bf16[1408,1024]{1,0:T(8,128)(2,1)} %down_ref.1) | copy-start | bytes 8650756
  135.2 23.9 %collective-permute-start = (bf16[512,1024]{1,0:T(8,128)(2,1)}, bf16[512,1024]{1,0:T(8,128)(2,1)}, u32[]{:S(2)}, u32[]{:S(2)}) collective-permute-start(bf16[512,1024]{1,0:T(8,128)(2,1)} %get-tuple-element.57), channel_id=1, source_target_pairs={{0,1},{1,0},{2,3},{3,2},{4,5},{5,4},{6,7},{7,6},{8,9},{9,8},{10,11... | collective-permute-start | bytes 3145736 | tf_op jit(solution)/shard_map/ppermute | solution.py:1244
  140.1 2.4 copy-start
  142.5 4.8 %copy-start.6 = (bf16[2,512,1408]{2,1,0:T(8,128)(2,1)S(1)}, bf16[2,512,1408]{2,1,0:T(8,128)(2,1)}, u32[]{:S(2)}) copy-start(bf16[2,512,1408]{2,1,0:T(8,128)(2,1)} %get-tuple-element.82) | copy-start | bytes 8650756
  142.5 4.8 %copy-start.7 = (bf16[512,1024]{1,0:T(8,128)(2,1)S(1)}, bf16[512,1024]{1,0:T(8,128)(2,1)}, u32[]{:S(2)}) copy-start(bf16[512,1024]{1,0:T(8,128)(2,1)} %get-tuple-element.83) | copy-start | bytes 3145732
  147.3 11.8 %copy-start.4 = (f32[512,1024]{1,0:T(8,128)S(1)}, f32[512,1024]{1,0:T(8,128)}, u32[]{:S(2)}) copy-start(f32[512,1024]{1,0:T(8,128)} %get-tuple-element.56) | copy-start | bytes 6291460
  159.1 2.9 copy-start.8
  161.0 1.0 copy-start.1
  325.8 80.2 %copy-start.3 = (bf16[512,1024]{1,0:T(8,128)(2,1)S(1)}, bf16[512,1024]{1,0:T(8,128)(2,1)}, u32[]{:S(2)}) copy-start(bf16[512,1024]{1,0:T(8,128)(2,1)} %get-tuple-element.76.refs_2_) | copy-start | bytes 3145732
  325.8 80.2 %copy-start.5 = (bf16[1,512,512]{2,1,0:T(8,128)(2,1)S(1)}, bf16[1,512,512]{2,1,0:T(8,128)(2,1)}, u32[]{:S(2)}) copy-start(bf16[1,512,512]{2,1,0:T(8,128)(2,1)} %get-tuple-element.62) | copy-start | bytes 1572868
Sparse Core Ops, SparseCore 0:
  163.9 248.9 all-reduce.2

commit v2 on v1

--- a/solution.py
+++ b/solution.py
@@ -296,7 +296,7 @@
         probs = jnp.exp2(dot_nt(q_ref[...], k_ref[span, :])).astype(low)
         acc_ref[...] += dot_nn(probs, v_ref[span, :])
 
-    walk(begin, end, step, 2048)
+    walk(begin, end, step, 4096)
     total = acc_ref[...]
     row_sum = total[:, HD : HD + 1]
     exact = total / row_sum
@@ -667,13 +667,31 @@
     )
 
 
+def peer(head, step, heads):
+    if heads & (heads - 1):
+        return lax.rem(head + step, heads)
+    to = 0
+    bit = 1
+    while bit < heads:
+        mine = lax.rem(head // bit, 2)
+        to = to + bit * (1 - mine if step & bit else mine)
+        bit *= 2
+    return to
+
+
+def origin(head, step, heads):
+    if heads & (heads - 1):
+        return lax.rem(head + heads - step, heads)
+    return peer(head, step, heads)
+
+
 def greet(heads, ranks, head, rank, with_ranks, tensor=1):
     barrier = pltpu.get_barrier_semaphore()
     for step in range(1, tensor):
         side = lax.rem(lax.axis_index("tensor") + step, tensor)
         pl.semaphore_signal(barrier, inc=1, device_id={"tensor": side}, device_id_type=MESH)
     for step in range(1, heads):
-        place = lax.rem(head + step, heads) * ranks + rank
+        place = peer(head, step, heads) * ranks + rank
         pl.semaphore_signal(barrier, inc=1, device_id={"dp": place}, device_id_type=MESH)
     if with_ranks:
         for step in range(1, ranks):
@@ -704,9 +722,9 @@
         )
         copy.start()
         onward.append(copy)
-    firsts = []
-    for step in range(1, heads):
-        to = lax.rem(head + step, heads)
+    firsts = {}
+    for step in reversed(range(1, heads)):
+        to = peer(head, step, heads)
         at = to * ranks + rank
         first = remote(
             message_ref.at[to, pl.ds(0, size)], kv_ref.at[rank, head],
@@ -718,7 +736,7 @@
         )
         first.start()
         second.start()
-        firsts.append((first, second))
+        firsts[step] = (first, second)
     mine = [
         pltpu.make_async_copy(message_ref.at[head, pl.ds(0, size)], kv_ref.at[rank, head], local.at[0]),
         pltpu.make_async_copy(message_ref.at[head, pl.ds(size, rest)], query_ref.at[head], local.at[1]),
@@ -736,11 +754,11 @@
             onward.append(copy)
 
     forward(0, head, message_ref.at[head, pl.ds(0, size)])
-    for step in range(1, heads):
-        source = lax.rem(head + heads - step, heads)
-        firsts[step - 1][0].wait_recv()
+    for step in reversed(range(1, heads)):
+        source = origin(head, step, heads)
+        firsts[step][0].wait_recv()
         forward(step, source, kv_ref.at[rank, source])
-    for first, second in firsts:
+    for first, second in firsts.values():
         first.wait_send()
         second.wait()
     for copy in mine + onward:
@@ -792,8 +810,8 @@
     rank = lax.rem(place, ranks)
     greet(heads, ranks, head, rank, False, shares_ref.shape[0] + 1)
     copies = []
-    for step in range(1, heads):
-        to = lax.rem(head + step, heads)
+    for step in reversed(range(1, heads)):
+        to = peer(head, step, heads)
         copies.append(
             remote(
                 message_ref.at[to], landed_ref.at[head], send.at[step], recv.at[step],
@@ -836,12 +854,12 @@
         to = lax.rem(side + step, tensor)
         pl.semaphore_signal(barrier, inc=1, device_id={"tensor": to}, device_id_type=MESH)
     for step in range(1, heads):
-        to = lax.rem(head + step, heads) * ranks + rank
+        to = peer(head, step, heads) * ranks + rank
         pl.semaphore_signal(barrier, inc=1, device_id={"dp": to}, device_id_type=MESH)
     pl.semaphore_wait(barrier, heads + tensor - 2)
     copies = []
     for step in range(1, heads):
-        to = lax.rem(head + step, heads)
+        to = peer(head, step, heads)
         copies.append(
             remote(
                 message_ref.at[to], landed_ref.at[0, head], send.at[step], recv.at[step],
@@ -865,7 +883,7 @@
 
     relay(0, head, message_ref.at[head])
     for step in range(1, heads):
-        source = lax.rem(head + heads - step, heads)
+        source = origin(head, step, heads)
         copies[step - 1].wait_recv()
         relay(step, source, landed_ref.at[0, source])
     for copy in copies:
@@ -1122,11 +1140,11 @@
     head = place // ranks
     rank = lax.rem(place, ranks)
     greet(heads, ranks, head, rank, True)
-    order = list(range(1, heads)) + [0]
+    order = list(reversed(range(heads)))
     pieces = {}
     copies = []
     for step in order:
-        to = lax.rem(head + step, heads)
+        to = peer(head, step, heads)
         for other in range(1, ranks):
             partner = lax.rem(rank + other, ranks)
             pieces[step, other] = remote(
@@ -1149,7 +1167,7 @@
             )
         copies[-1].start()
     for step in order:
-        to = lax.rem(head + step, heads)
+        to = peer(head, step, heads)
         total = kv_ref[rank, to].astype(wide)
         for other in range(1, ranks):
             pieces[step, other].wait_recv()
@@ -1290,9 +1308,8 @@
     qkv_sum, small, input_others = total_sums([grad_qkv], small, input_part, dp, tensor)
     grad_input = share_of(grad_middle) + share_sum(input_part, input_others)
     flat = lambda x: x.reshape(-1, x.shape[-1])
-    qkv_wide, out_wide, gateup_wide, down_wide = widen(
-        [flat(qkv_sum), out_sum, flat(early[0]), early[1]]
-    )
+    (qkv_wide,) = widen([flat(qkv_sum)])
+    gateup_wide, out_wide, down_wide = widen([flat(early[0]), out_sum, early[1]])
     count = 2 * depth // LANES
     gains = small[:count].reshape(2, depth)
     head_gains = small[count : count + 2, :HD] + small[count : count + 2, HD:]

time: 443 us -> 439 us (level)
    pallas_call x1, Pallas kernels: 73.4 us -> 67.5 us  [backward_attention(): pl.pallas_call(backward_kernel, grid_spec=pltpu.PrefetchScalarGridSpec(nu...]
    pallas_call x1, Pallas kernels: 17.8 us -> 23.3 us  [exchange(): pl.pallas_call(functools.partial(exchange_kernel, ranks=ranks), in_specs=...]
    pallas_call x1 -> x2, Pallas kernels: 14.3 us -> 18.1 us  [widen(): pl.pallas_call(widen_kernel, grid=(steps,), in_specs=specs, out_specs=tup...]
  transfers between devices with their start and end apart: 2 -> 2, of which waited for: 2 -> 1; matrix products, arithmetic and copies ran while one was open for 6% -> 6% of each run, Pallas kernels for 54% -> 57%
where the time goes in v2:
time: 439 us; the launch traced here: 431 us
  Pallas kernels  377 us (86%)
  matrix products  16.2 us (4%)
  between operations  14.4 us (3%)
  other arithmetic  8.25 us (2%)
  local copies, waits for them, and re-layouts  7.31 us (2%)
  waiting for transfers between devices  7.03 us (2%)
    pallas_call x1, Pallas kernels, total_sums(): pl.pallas_call(functools.partial(total_kernel, arrays=len(arrays), chunks...  76.6 us
    pallas_call x1, Pallas kernels, backward_attention(): pl.pallas_call(backward_kernel, grid_spec=pltpu.PrefetchScalarGridSpec(nu...  67.5 us
    pallas_call x1, Pallas kernels, collect(): pl.pallas_call(functools.partial(collect_kernel, ranks=ranks), in_specs=[...  55 us
    pallas_call x1, Pallas kernels, spread(): pl.pallas_call(functools.partial(spread_kernel, ranks=ranks), in_specs=[A...  39.7 us
    pallas_call x1, Pallas kernels, forward_attention(): pl.pallas_call(forward_kernel, grid=(heads,), in_specs=[SCALARS, WHOLE, f...  35.6 us
    pallas_call x1, Pallas kernels, exchange(): pl.pallas_call(functools.partial(exchange_kernel, ranks=ranks), in_specs=...  23.3 us
    pallas_call x1, Pallas kernels, share_out(): pl.pallas_call(functools.partial(share_out_kernel, ranks=ranks, tensor=te...  20 us
    pallas_call x2, Pallas kernels, widen(): pl.pallas_call(widen_kernel, grid=(steps,), in_specs=specs, out_specs=tup...  18.1 us
  transfers between devices with their start and end apart: 2, of which 1 were waited for; matrix products, arithmetic and copies ran while one was open for 6% of the time, Pallas kernels for 57%

profile of v2, /device:TPU:8, one launch (start us, length us, event | category | flops | bytes accessed | tf_op | source)
XLA Modules:
  0.0 431.1 jit_solution(9302409841072133260)
XLA Ops:
  7.2 0.0 all-reduce.3.cloned.1.call-start
  7.2 0.7 convert_element_type.38
  7.9 2.5 fusion.4
  10.4 7.4 %shard_map.239 = (bf16[8,784,128]{2,1,0:T(8,128)(2,1)}, f32[512,512]{1,0:T(8,128)}, f32[512,512]{1,0:T(8,128)}, bf16[512,1024]{1,0:T(8,128)(2,1)}) custom-call(bf16[512,1024]{1,0:T(8,128)(2,1)} %tokens_ref.5, bf16[3,1024,512]{2,1,0:T(8,128)(2,1)} %w_ref.7, f32[1,1024]{1,0:T(1,128)} %bitcast.43, f32[1,64]{1,0:T(1,128)} %bitcast.48, f32[1,64]{1,0:T(1,128)} %bitcast.50, ...), custom_call_target="tpu_custom_call" | custom-call | tf_op jit(solution)/shard_map/pallas_call | solution.py:188
  17.7 39.7 %shard_map.240 = (bf16[2,8,528,128]{3,2,1,0:T(8,128)(2,1)}, bf16[8,256,128]{2,1,0:T(8,128)(2,1)}, bf16[1,512,1024]{2,1,0:T(8,128)(2,1)}) custom-call(bf16[8,784,128]{2,1,0:T(8,128)(2,1)} %get-tuple-element.49.message_ref, bf16[512,1024]{1,0:T(8,128)(2,1)} %w_ref.6), custom_call_target="tpu_custom_call" | custom-call | tf_op jit(solution)/shard_map/pallas_call | solution.py:771
  57.5 35.6 %shard_map.241 = (bf16[8192,128]{1,0:T(8,128)(2,1)}, bf16[8192,128]{1,0:T(8,128)(2,1)}, bf16[4096,128]{1,0:T(8,128)(2,1)}, f32[4096,128]{1,0:T(8,128)}, bf16[8,256,128]{2,1,0:T(8,128)(2,1)}, /*index=5*/s32[2,16]{1,0:T(2,128)}) custom-call(f32[2,8]{1,0:T(2,128)} %bias_ref.1, bf16[2,8,528,128]{3,2,1,0:T(8,128)(2,1)} %get-tuple-element.50.kv_ref, ...), custom_call_target="tpu_custom_call" | custom-call | tf_op jit(solution)/shard_map/pallas_call | solution.py:313
  93.1 20.0 %shard_map.242.landed_ref = bf16[2,8,256,128]{3,2,1,0:T(8,128)(2,1)} custom-call(bf16[8,256,128]{2,1,0:T(8,128)(2,1)} %get-tuple-element.52.message_ref), custom_call_target="tpu_custom_call" | custom-call | tf_op jit(solution)/shard_map/pallas_call | solution.py:899
  113.1 0.0 copy-start.2
  113.1 17.9 %shard_map.243 = (bf16[512,512]{1,0:T(8,128)(2,1)}, f32[512,1024]{1,0:T(8,128)}, bf16[512,1024]{1,0:T(8,128)(2,1)}, bf16[512,1408]{1,0:T(8,128)(2,1)}, bf16[2,51...) custom-call(bf16[2,8,256,128]{3,2,1,0:T(8,128)(2,1)} %shard_map.242.landed_ref, ...), custom_call_target="tpu_custom_call" | custom-call | tf_op jit(solution)/shard_map/pallas_call | solution.py:514
  131.0 0.6 collective-permute-start
  131.6 0.0 copy-done.2
  131.6 4.5 %convolution_convert_fusion.2.part_ref = bf16[512,1024]{1,0:T(8,128)(2,1)} fusion(bf16[512,1408]{1,0:T(8,128)(2,1)} %get-tuple-element.57, bf16[1408,1024]{1,0:T(8,128)(2,1)S(1)} %copy-done.2), kind=kOutput, calls=%fused_computation.3 | convolution fusion | flops 1476919296 | bytes 5373952 | tf_op jit(solution)/shard_map/dot_general | solution.py:1286
  136.1 0.0 copy-start
  136.1 2.4 copy.27
  138.5 0.0 copy-done
  138.5 0.0 copy-start.7
  138.5 0.0 copy-start.8
  138.5 4.8 %convolution_convert_fusion.1 = bf16[1408,1024]{1,0:T(8,128)(2,1)} fusion(bf16[512,1408]{1,0:T(8,128)(2,1)} %get-tuple-element.57, bf16[512,1024]{1,0:T(8,128)(2,1)S(1)} %copy-done), kind=kOutput, calls=%fused_computation.1 | convolution fusion | flops 1477836800 | bytes 5373952 | tf_op jit(solution)/shard_map/tf,te->fe/dot_general | solution.py:1283
  143.3 0.0 copy-done.7
  143.3 0.0 copy-done.8
  143.3 0.0 copy-start.4
  143.3 5.1 %convolution_convert_fusion = bf16[2,1408,1024]{1,2,0:T(8,128)(2,1)} fusion(bf16[2,512,1408]{2,1,0:T(8,128)(2,1)S(1)} %copy-done.7, bf16[512,1024]{1,0:T(8,128)(2,1)S(1)} %copy-done.8), kind=kOutput, calls=%fused_computation | convolution fusion | flops 2955673600 | bytes 9699328 | tf_op jit(solution)/shard_map/td,ktf->kdf/dot_general | solution.py:1284
  148.4 7.0 %collective-permute-done = bf16[512,1024]{1,0:T(8,128)(2,1)} collective-permute-done((bf16[512,1024]{1,0:T(8,128)(2,1)}, bf16[512,1024]{1,0:T(8,128)(2,1)}, u32[]{:S(2)}, u32[]{:S(2)}) %collective-permute-start) | collective-permute-done | bytes 1048608 | tf_op jit(solution)/shard_map/ppermute | solution.py:1262
  155.4 0.0 copy-done.4
  155.4 0.0 copy-start.9
  155.4 1.9 fusion.5
  157.3 0.0 copy-start.1
  157.4 1.0 copy-done.1
  158.4 0.0 copy-done.9
  158.4 1.7 convolution_convert_fusion.3
  160.1 0.0 all-reduce.3.cloned.1.call-update
  160.1 0.9 slice.29
  160.9 0.6 dynamic-slice_bitcast_fusion.ids_ref
  161.6 3.7 shard_map.244.message_ref
  165.2 23.3 %shard_map.245 = (bf16[8,256,128]{2,1,0:T(8,128)(2,1)}, bf16[1,512,512]{2,1,0:T(8,128)(2,1)}) custom-call(bf16[8,256,128]{2,1,0:T(8,128)(2,1)} %shard_map.244.message_ref, bf16[512,1024]{1,0:T(8,128)(2,1)} %convolution_convert_fusion.2.part_ref), custom_call_target="tpu_custom_call" | custom-call | tf_op jit(solution)/shard_map/pallas_call | solution.py:833
  188.5 67.5 %shard_map.246 = (bf16[2,8,512,128]{3,2,1,0:T(8,128)(2,1)}, bf16[8,256,128]{2,1,0:T(8,128)(2,1)}, f32[2,8,128]{2,1,0:T(8,128)}) custom-call(s32[2,16]{1,0:T(2,128)} %get-tuple-element.62.runs_ref, bf16[8192,128]{1,0:T(8,128)(2,1)} %get-tuple-element.63.k_ref, bf16[8192,128]{1,0:T(8,128)(2,1)} %get-tuple-element.64.v_ref, ...), custom_call_target="tpu_custom_call" | custom-call | tf_op jit(solution)/shard_map/pallas_call | solution.py:414
  256.1 55.0 %shard_map.247.landed_ref = bf16[8,768,128]{2,1,0:T(8,128)(2,1)} custom-call(bf16[2,8,512,128]{3,2,1,0:T(8,128)(2,1)} %get-tuple-element.68.kv_ref, bf16[8,256,128]{2,1,0:T(8,128)(2,1)} %get-tuple-element.69.query_ref), custom_call_target="tpu_custom_call" | custom-call | tf_op jit(solution)/shard_map/pallas_call | solution.py:1199
  311.1 12.7 %shard_map.248 = (bf16[3,1024,512]{2,1,0:T(8,128)(2,1)}, bf16[512,1024]{1,0:T(8,128)(2,1)}, f32[24,128]{1,0:T(8,128)}) custom-call(bf16[8,768,128]{2,1,0:T(8,128)(2,1)} %shard_map.247.landed_ref, f32[512,512]{1,0:T(8,128)} %get-tuple-element.70.query_ref, f32[512,512]{1,0:T(8,128)} %get-tuple-element.71.key_ref, f32[1,64]{1,0:T(1,128)} %bitcast.49, ...), custom_call_target="tpu_custom_call" | custom-call | tf_op jit(solution)/shard_map/pallas_call | solution.py:625
  323.8 76.6 %shard_map.249 = (bf16[3,1024,512]{2,1,0:T(8,128)(2,1)}, f32[24,128]{1,0:T(8,128)}, bf16[1,512,512]{2,1,0:T(8,128)(2,1)}) custom-call(bf16[3,1024,512]{2,1,0:T(8,128)(2,1)} %get-tuple-element.76.refs_0_, f32[24,128]{1,0:T(8,128)} %get-tuple-element.77.refs_1_, bf16[512,1024]{1,0:T(8,128)(2,1)} %get-tuple-element.75.refs_2_), custom_call_target="tpu_custom_call" | custom-call | tf_op jit(solution)/shard_map/pallas_call | solution.py:1110
  400.3 0.7 slice.36
  401.0 0.0 copy-start.6
  401.0 0.0 copy-start.3
  401.0 0.0 copy-start.5
  401.0 6.7 %shard_map.250 = f32[3072,512]{1,0:T(8,128)} custom-call(bf16[3072,512]{1,0:T(8,128)(2,1)} %bitcast.42), custom_call_target="tpu_custom_call" | custom-call | tf_op jit(solution)/shard_map/pallas_call | solution.py:653
  407.8 0.6 constant_dynamic-slice_fusion
  408.4 0.0 copy-done.6
  408.4 0.1 slice_add_fusion
  408.5 0.5 slice_bitcast_fusion.2
  409.0 0.6 slice_bitcast_fusion
  409.6 0.0 copy-done.3
  409.6 0.0 copy-done.5
  409.6 3.1 fusion
  412.7 0.0 all-reduce.3.cloned.1.call-done
  412.7 11.3 %shard_map.251 = (f32[2048,1408]{1,0:T(8,128)}, f32[512,1024]{1,0:T(8,128)}, f32[1408,1024]{1,0:T(8,128)}) custom-call(bf16[2048,1408]{1,0:T(8,128)(2,1)} %get-tuple-element.87.refs_0_, bf16[512,1024]{1,0:T(8,128)(2,1)} %get-tuple-element.88.refs_1_, bf16[1408,1024]{1,0:T(8,128)(2,1)} %get-tuple-element.89.refs_2_), custom_call_target="tpu_custom_call" | custom-call | tf_op jit(solution)/shard_map/pallas_call | solution.py:653
Async XLA Ops:
  7.2 405.5 %all-reduce.3.cloned.1.call-start = ((), (), s32[]{:S(2)}) async-start(), calls=%async_computation | async-start | bytes 19398656 | tf_op jit(solution)/shard_map/psum | solution.py:1294
  113.1 18.5 %copy-start.2 = (bf16[1408,1024]{1,0:T(8,128)(2,1)S(1)}, bf16[1408,1024]{1,0:T(8,128)(2,1)}, u32[]{:S(2)}) copy-start(bf16[1408,1024]{1,0:T(8,128)(2,1)} %down_ref.1) | copy-start | bytes 8650756
  131.0 24.4 %collective-permute-start = (bf16[512,1024]{1,0:T(8,128)(2,1)}, bf16[512,1024]{1,0:T(8,128)(2,1)}, u32[]{:S(2)}, u32[]{:S(2)}) collective-permute-start(bf16[512,1024]{1,0:T(8,128)(2,1)} %get-tuple-element.56), channel_id=1, source_target_pairs={{0,1},{1,0},{2,3},{3,2},{4,5},{5,4},{6,7},{7,6},{8,9},{9,8},{10,11... | collective-permute-start | bytes 3145736 | tf_op jit(solution)/shard_map/ppermute | solution.py:1262
  136.1 2.4 copy-start
  138.5 4.8 %copy-start.7 = (bf16[2,512,1408]{2,1,0:T(8,128)(2,1)S(1)}, bf16[2,512,1408]{2,1,0:T(8,128)(2,1)}, u32[]{:S(2)}) copy-start(bf16[2,512,1408]{2,1,0:T(8,128)(2,1)} %get-tuple-element.80) | copy-start | bytes 8650756
  138.5 4.8 %copy-start.8 = (bf16[512,1024]{1,0:T(8,128)(2,1)S(1)}, bf16[512,1024]{1,0:T(8,128)(2,1)}, u32[]{:S(2)}) copy-start(bf16[512,1024]{1,0:T(8,128)(2,1)} %get-tuple-element.81) | copy-start | bytes 3145732
  143.3 12.1 %copy-start.4 = (f32[512,1024]{1,0:T(8,128)S(1)}, f32[512,1024]{1,0:T(8,128)}, u32[]{:S(2)}) copy-start(f32[512,1024]{1,0:T(8,128)} %get-tuple-element.55) | copy-start | bytes 6291460
  155.4 2.9 copy-start.9
  157.3 1.0 copy-start.1
  401.0 7.4 %copy-start.6 = (f32[24,128]{1,0:T(8,128)S(1)}, f32[24,128]{1,0:T(8,128)}, u32[]{:S(2)}) copy-start(f32[24,128]{1,0:T(8,128)} %get-tuple-element.86) | copy-start | bytes 36868
  401.0 8.6 %copy-start.3 = (bf16[512,1024]{1,0:T(8,128)(2,1)S(1)}, bf16[512,1024]{1,0:T(8,128)(2,1)}, u32[]{:S(2)}) copy-start(bf16[512,1024]{1,0:T(8,128)(2,1)} %get-tuple-element.75.refs_2_) | copy-start | bytes 3145732
  401.0 8.6 %copy-start.5 = (bf16[1,512,512]{2,1,0:T(8,128)(2,1)S(1)}, bf16[1,512,512]{2,1,0:T(8,128)(2,1)}, u32[]{:S(2)}) copy-start(bf16[1,512,512]{2,1,0:T(8,128)(2,1)} %get-tuple-element.61) | copy-start | bytes 1572868
Sparse Core Ops, SparseCore 0:
  160.2 251.6 all-reduce.2

commit v3 on v2

--- a/solution.py
+++ b/solution.py
@@ -443,7 +443,7 @@
 def columns_of(width):
     if width % LANES:
         return [(0, width)]
-    return [(at, min(2 * LANES, width - at)) for at in range(0, width, 2 * LANES)]
+    return [(at, min(4 * LANES, width - at)) for at in range(0, width, 4 * LANES)]
 
 
 def mlp_kernel(

time: 439 us -> 442 us (level)
  waiting for transfers between devices: 7.03 us -> 12 us
    psum x1, waiting for transfers between devices: 0.01 us -> 4.76 us  [shards(): early = lax.psum((*early, grad_out.astype(low)), 'dp')]
  transfers between devices with their start and end apart: 2 -> 2, of which waited for: 1 -> 2; matrix products, arithmetic and copies ran while one was open for 6% -> 5% of each run, Pallas kernels for 57% -> 56%
where the time goes in v3:
time: 442 us; the launch traced here: 434 us
  Pallas kernels  375 us (85%)
  matrix products  15.9 us (4%)
  between operations  14.6 us (3%)
  waiting for transfers between devices  12 us (3%)
  other arithmetic  8.25 us (2%)
  local copies, waits for them, and re-layouts  7.31 us (2%)
    pallas_call x1, Pallas kernels, total_sums(): pl.pallas_call(functools.partial(total_kernel, arrays=len(arrays), chunks...  79.9 us
    pallas_call x1, Pallas kernels, backward_attention(): pl.pallas_call(backward_kernel, grid_spec=pltpu.PrefetchScalarGridSpec(nu...  64.1 us
    pallas_call x1, Pallas kernels, collect(): pl.pallas_call(functools.partial(collect_kernel, ranks=ranks), in_specs=[...  55.3 us
    pallas_call x1, Pallas kernels, spread(): pl.pallas_call(functools.partial(spread_kernel, ranks=ranks), in_specs=[A...  39.7 us
    pallas_call x1, Pallas kernels, forward_attention(): pl.pallas_call(forward_kernel, grid=(heads,), in_specs=[SCALARS, WHOLE, f...  33.7 us
    pallas_call x1, Pallas kernels, share_out(): pl.pallas_call(functools.partial(share_out_kernel, ranks=ranks, tensor=te...  23.2 us
    pallas_call x1, Pallas kernels, exchange(): pl.pallas_call(functools.partial(exchange_kernel, ranks=ranks), in_specs=...  21.3 us
    pallas_call x2, Pallas kernels, widen(): pl.pallas_call(widen_kernel, grid=(steps,), in_specs=specs, out_specs=tup...  18.1 us
  transfers between devices with their start and end apart: 2, of which 2 were waited for; matrix products, arithmetic and copies ran while one was open for 5% of the time, Pallas kernels for 56%

profile of v3, /device:TPU:8, one launch (start us, length us, event | category | flops | bytes accessed | tf_op | source)
XLA Modules:
  0.0 433.5 jit_solution(1309931142300791287)
XLA Ops:
  7.2 0.0 all-reduce.3.cloned.1.call-start
  7.2 0.7 convert_element_type.38
  7.9 2.5 fusion.4
  10.4 7.4 %shard_map.239 = (bf16[8,784,128]{2,1,0:T(8,128)(2,1)}, f32[512,512]{1,0:T(8,128)}, f32[512,512]{1,0:T(8,128)}, bf16[512,1024]{1,0:T(8,128)(2,1)}) custom-call(bf16[512,1024]{1,0:T(8,128)(2,1)} %tokens_ref.5, bf16[3,1024,512]{2,1,0:T(8,128)(2,1)} %w_ref.7, f32[1,1024]{1,0:T(1,128)} %bitcast.43, f32[1,64]{1,0:T(1,128)} %bitcast.48, f32[1,64]{1,0:T(1,128)} %bitcast.50, ...), custom_call_target="tpu_custom_call" | custom-call | tf_op jit(solution)/shard_map/pallas_call | solution.py:188
  17.7 39.7 %shard_map.240 = (bf16[2,8,528,128]{3,2,1,0:T(8,128)(2,1)}, bf16[8,256,128]{2,1,0:T(8,128)(2,1)}, bf16[1,512,1024]{2,1,0:T(8,128)(2,1)}) custom-call(bf16[8,784,128]{2,1,0:T(8,128)(2,1)} %get-tuple-element.49.message_ref, bf16[512,1024]{1,0:T(8,128)(2,1)} %w_ref.6), custom_call_target="tpu_custom_call" | custom-call | tf_op jit(solution)/shard_map/pallas_call | solution.py:771
  57.5 33.7 %shard_map.241 = (bf16[8192,128]{1,0:T(8,128)(2,1)}, bf16[8192,128]{1,0:T(8,128)(2,1)}, bf16[4096,128]{1,0:T(8,128)(2,1)}, f32[4096,128]{1,0:T(8,128)}, bf16[8,256,128]{2,1,0:T(8,128)(2,1)}, /*index=5*/s32[2,16]{1,0:T(2,128)}) custom-call(f32[2,8]{1,0:T(2,128)} %bias_ref.1, bf16[2,8,528,128]{3,2,1,0:T(8,128)(2,1)} %get-tuple-element.50.kv_ref, ...), custom_call_target="tpu_custom_call" | custom-call | tf_op jit(solution)/shard_map/pallas_call | solution.py:313
  91.2 23.2 %shard_map.242.landed_ref = bf16[2,8,256,128]{3,2,1,0:T(8,128)(2,1)} custom-call(bf16[8,256,128]{2,1,0:T(8,128)(2,1)} %get-tuple-element.52.message_ref), custom_call_target="tpu_custom_call" | custom-call | tf_op jit(solution)/shard_map/pallas_call | solution.py:899
  114.4 0.0 copy-start.2
  114.4 17.0 %shard_map.243 = (bf16[512,512]{1,0:T(8,128)(2,1)}, f32[512,1024]{1,0:T(8,128)}, bf16[512,1024]{1,0:T(8,128)(2,1)}, bf16[512,1408]{1,0:T(8,128)(2,1)}, bf16[2,51...) custom-call(bf16[2,8,256,128]{3,2,1,0:T(8,128)(2,1)} %shard_map.242.landed_ref, ...), custom_call_target="tpu_custom_call" | custom-call | tf_op jit(solution)/shard_map/pallas_call | solution.py:514
  131.5 0.6 collective-permute-start
  132.0 0.0 copy-done.2
  132.1 4.1 convolution_convert_fusion.2.part_ref
  136.2 0.0 copy-start
  136.2 2.4 copy.27
  138.5 0.0 copy-done
  138.5 0.0 copy-start.7
  138.6 0.0 copy-start.8
  138.6 4.8 %convolution_convert_fusion.1 = bf16[1408,1024]{1,0:T(8,128)(2,1)} fusion(bf16[512,1408]{1,0:T(8,128)(2,1)} %get-tuple-element.57, bf16[512,1024]{1,0:T(8,128)(2,1)S(1)} %copy-done), kind=kOutput, calls=%fused_computation.1 | convolution fusion | flops 1477836800 | bytes 5373952 | tf_op jit(solution)/shard_map/tf,te->fe/dot_general | solution.py:1283
  143.3 0.0 copy-done.7
  143.3 0.0 copy-done.8
  143.3 0.0 copy-start.4
  143.3 5.3 %convolution_convert_fusion = bf16[2,1408,1024]{1,2,0:T(8,128)(2,1)} fusion(bf16[2,512,1408]{2,1,0:T(8,128)(2,1)S(1)} %copy-done.7, bf16[512,1024]{1,0:T(8,128)(2,1)S(1)} %copy-done.8), kind=kOutput, calls=%fused_computation | convolution fusion | flops 2955673600 | bytes 9699328 | tf_op jit(solution)/shard_map/td,ktf->kdf/dot_general | solution.py:1284
  148.7 7.2 %collective-permute-done = bf16[512,1024]{1,0:T(8,128)(2,1)} collective-permute-done((bf16[512,1024]{1,0:T(8,128)(2,1)}, bf16[512,1024]{1,0:T(8,128)(2,1)}, u32[]{:S(2)}, u32[]{:S(2)}) %collective-permute-start) | collective-permute-done | bytes 1048608 | tf_op jit(solution)/shard_map/ppermute | solution.py:1262
  155.9 0.0 copy-done.4
  155.9 0.0 copy-start.9
  155.9 1.9 fusion.5
  157.8 0.0 copy-start.1
  157.8 1.0 copy-done.1
  158.8 0.0 copy-done.9
  158.8 1.7 convolution_convert_fusion.3
  160.5 0.0 all-reduce.3.cloned.1.call-update
  160.6 0.9 slice.29
  161.4 0.6 dynamic-slice_bitcast_fusion.ids_ref
  162.0 3.7 shard_map.244.message_ref
  165.7 21.3 %shard_map.245 = (bf16[8,256,128]{2,1,0:T(8,128)(2,1)}, bf16[1,512,512]{2,1,0:T(8,128)(2,1)}) custom-call(bf16[8,256,128]{2,1,0:T(8,128)(2,1)} %shard_map.244.message_ref, bf16[512,1024]{1,0:T(8,128)(2,1)} %convolution_convert_fusion.2.part_ref), custom_call_target="tpu_custom_call" | custom-call | tf_op jit(solution)/shard_map/pallas_call | solution.py:833
  187.0 64.1 %shard_map.246 = (bf16[2,8,512,128]{3,2,1,0:T(8,128)(2,1)}, bf16[8,256,128]{2,1,0:T(8,128)(2,1)}, f32[2,8,128]{2,1,0:T(8,128)}) custom-call(s32[2,16]{1,0:T(2,128)} %get-tuple-element.62.runs_ref, bf16[8192,128]{1,0:T(8,128)(2,1)} %get-tuple-element.63.k_ref, bf16[8192,128]{1,0:T(8,128)(2,1)} %get-tuple-element.64.v_ref, ...), custom_call_target="tpu_custom_call" | custom-call | tf_op jit(solution)/shard_map/pallas_call | solution.py:414
  251.1 55.3 %shard_map.247.landed_ref = bf16[8,768,128]{2,1,0:T(8,128)(2,1)} custom-call(bf16[2,8,512,128]{3,2,1,0:T(8,128)(2,1)} %get-tuple-element.68.kv_ref, bf16[8,256,128]{2,1,0:T(8,128)(2,1)} %get-tuple-element.69.query_ref), custom_call_target="tpu_custom_call" | custom-call | tf_op jit(solution)/shard_map/pallas_call | solution.py:1199
  306.5 11.3 %shard_map.248 = (bf16[3,1024,512]{2,1,0:T(8,128)(2,1)}, bf16[512,1024]{1,0:T(8,128)(2,1)}, f32[24,128]{1,0:T(8,128)}) custom-call(bf16[8,768,128]{2,1,0:T(8,128)(2,1)} %shard_map.247.landed_ref, f32[512,512]{1,0:T(8,128)} %get-tuple-element.70.query_ref, f32[512,512]{1,0:T(8,128)} %get-tuple-element.71.key_ref, f32[1,64]{1,0:T(1,128)} %bitcast.49, ...), custom_call_target="tpu_custom_call" | custom-call | tf_op jit(solution)/shard_map/pallas_call | solution.py:625
  317.8 79.9 %shard_map.249 = (bf16[3,1024,512]{2,1,0:T(8,128)(2,1)}, f32[24,128]{1,0:T(8,128)}, bf16[1,512,512]{2,1,0:T(8,128)(2,1)}) custom-call(bf16[3,1024,512]{2,1,0:T(8,128)(2,1)} %get-tuple-element.76.refs_0_, f32[24,128]{1,0:T(8,128)} %get-tuple-element.77.refs_1_, bf16[512,1024]{1,0:T(8,128)(2,1)} %get-tuple-element.75.refs_2_), custom_call_target="tpu_custom_call" | custom-call | tf_op jit(solution)/shard_map/pallas_call | solution.py:1110
  397.7 0.7 slice.36
  398.4 0.0 copy-start.6
  398.4 0.0 copy-start.3
  398.4 0.0 copy-start.5
  398.4 6.7 %shard_map.250 = f32[3072,512]{1,0:T(8,128)} custom-call(bf16[3072,512]{1,0:T(8,128)(2,1)} %bitcast.42), custom_call_target="tpu_custom_call" | custom-call | tf_op jit(solution)/shard_map/pallas_call | solution.py:653
  405.2 0.6 constant_dynamic-slice_fusion
  405.8 0.0 copy-done.6
  405.8 0.1 slice_add_fusion
  405.9 0.5 slice_bitcast_fusion.2
  406.4 0.6 slice_bitcast_fusion
  407.0 0.0 copy-done.3
  407.0 0.0 copy-done.5
  407.0 3.1 fusion
  410.1 4.8 %all-reduce.3.cloned.1.call-done = (bf16[2048,1408]{1,0:T(8,128)(2,1)}, bf16[512,1024]{1,0:T(8,128)(2,1)}, bf16[1408,1024]{1,0:T(8,128)(2,1)}) async-done(((bf16[2048,1408]{1,0:T(8,128)(2,1)}, bf16[512,1024]{1,0:T(8,128)(2,1)}, bf16[1408,1024]{1,0:T(8,128)(2,1)}), (bf16[2048,1408]{1,0:T(8,128)(2,1)}, bf16[512,1024]{1,0:T(8,128)(2,1)}, bf16[1408,1024]{1,0:T(8,128)(2,1)})) %all-reduce.3.cloned.1.call-update) | async-done | bytes 9699344 | tf_op jit(solution)/shard_map/psum | solution.py:1294
  414.9 11.3 %shard_map.251 = (f32[2048,1408]{1,0:T(8,128)}, f32[512,1024]{1,0:T(8,128)}, f32[1408,1024]{1,0:T(8,128)}) custom-call(bf16[2048,1408]{1,0:T(8,128)(2,1)} %get-tuple-element.87.refs_0_, bf16[512,1024]{1,0:T(8,128)(2,1)} %get-tuple-element.88.refs_1_, bf16[1408,1024]{1,0:T(8,128)(2,1)} %get-tuple-element.89.refs_2_), custom_call_target="tpu_custom_call" | custom-call | tf_op jit(solution)/shard_map/pallas_call | solution.py:653
Async XLA Ops:
  7.2 407.7 %all-reduce.3.cloned.1.call-start = ((), (), s32[]{:S(2)}) async-start(), calls=%async_computation | async-start | bytes 19398656 | tf_op jit(solution)/shard_map/psum | solution.py:1294
  114.4 17.6 %copy-start.2 = (bf16[1408,1024]{1,0:T(8,128)(2,1)S(1)}, bf16[1408,1024]{1,0:T(8,128)(2,1)}, u32[]{:S(2)}) copy-start(bf16[1408,1024]{1,0:T(8,128)(2,1)} %down_ref.1) | copy-start | bytes 8650756
  131.5 24.4 %collective-permute-start = (bf16[512,1024]{1,0:T(8,128)(2,1)}, bf16[512,1024]{1,0:T(8,128)(2,1)}, u32[]{:S(2)}, u32[]{:S(2)}) collective-permute-start(bf16[512,1024]{1,0:T(8,128)(2,1)} %get-tuple-element.56), channel_id=1, source_target_pairs={{0,1},{1,0},{2,3},{3,2},{4,5},{5,4},{6,7},{7,6},{8,9},{9,8},{10,11... | collective-permute-start | bytes 3145736 | tf_op jit(solution)/shard_map/ppermute | solution.py:1262
  136.2 2.4 copy-start
  138.5 4.8 %copy-start.7 = (bf16[2,512,1408]{2,1,0:T(8,128)(2,1)S(1)}, bf16[2,512,1408]{2,1,0:T(8,128)(2,1)}, u32[]{:S(2)}) copy-start(bf16[2,512,1408]{2,1,0:T(8,128)(2,1)} %get-tuple-element.80) | copy-start | bytes 8650756
  138.6 4.8 %copy-start.8 = (bf16[512,1024]{1,0:T(8,128)(2,1)S(1)}, bf16[512,1024]{1,0:T(8,128)(2,1)}, u32[]{:S(2)}) copy-start(bf16[512,1024]{1,0:T(8,128)(2,1)} %get-tuple-element.81) | copy-start | bytes 3145732
  143.3 12.6 %copy-start.4 = (f32[512,1024]{1,0:T(8,128)S(1)}, f32[512,1024]{1,0:T(8,128)}, u32[]{:S(2)}) copy-start(f32[512,1024]{1,0:T(8,128)} %get-tuple-element.55) | copy-start | bytes 6291460
  155.9 2.9 copy-start.9
  157.8 1.0 copy-start.1
  398.4 7.4 %copy-start.6 = (f32[24,128]{1,0:T(8,128)S(1)}, f32[24,128]{1,0:T(8,128)}, u32[]{:S(2)}) copy-start(f32[24,128]{1,0:T(8,128)} %get-tuple-element.86) | copy-start | bytes 36868
  398.4 8.6 %copy-start.3 = (bf16[512,1024]{1,0:T(8,128)(2,1)S(1)}, bf16[512,1024]{1,0:T(8,128)(2,1)}, u32[]{:S(2)}) copy-start(bf16[512,1024]{1,0:T(8,128)(2,1)} %get-tuple-element.75.refs_2_) | copy-start | bytes 3145732
  398.4 8.6 %copy-start.5 = (bf16[1,512,512]{2,1,0:T(8,128)(2,1)S(1)}, bf16[1,512,512]{2,1,0:T(8,128)(2,1)}, u32[]{:S(2)}) copy-start(bf16[1,512,512]{2,1,0:T(8,128)(2,1)} %get-tuple-element.61) | copy-start | bytes 1572868
Sparse Core Ops, SparseCore 0:
  160.7 254.1 all-reduce.2
